TPU v7x, 32 devices: a whole 2x2x4 slice. The times are simulated.
32 devices in a mesh: fsdp: 16 (over z, x, core), tp: 2 (over y).
Axes of the slice: x: 2, y: 2, z: 4, core: 2. Of those that a mesh axis runs over, the one named last changes fastest.
Arguments:
- inputs: bfloat16 [32, 736, 1152], P('fsdp', 'tp'), may hold values from -6 to 6
- w_qkv: bfloat16 [3, 1152, 1152], P(None, 'fsdp', 'tp'), may hold values from -0.25 to 0.25
- w_out: bfloat16 [1152, 1152], P('tp', 'fsdp'), may hold values from -0.75 to 0.75
- w_up: bfloat16 [1152, 4304], P('fsdp', 'tp'), may hold values from -0.1875 to 0.1875
- w_down: bfloat16 [4304, 1152], P('tp', 'fsdp'), may hold values from -0.09375 to 0.09375
- norm_gains: float32 [2, 1152], replicated, may hold values from 0.1 to 1.9
- biases: float32 [6, 1152], replicated, may hold values from -3 to 3
- up_bias: float32 [4304], replicated, may hold values from -3 to 3
- cotangent: bfloat16 [32, 736, 1152], P('fsdp', 'tp'), may hold values from -6 to 6
Outputs:
- outputs: bfloat16 [32, 736, 1152], P('fsdp', 'tp')
- input_grad: float32 [32, 736, 1152], P('fsdp', 'tp')
- w_qkv_grad: float32 [3, 1152, 1152], P(None, 'fsdp', 'tp')
- w_out_grad: float32 [1152, 1152], P('tp', 'fsdp')
- w_up_grad: float32 [1152, 4304], P('fsdp', 'tp')
- w_down_grad: float32 [4304, 1152], P('tp', 'fsdp')
- norm_gains_grad: float32 [2, 1152], replicated
- biases_grad: float32 [6, 1152], replicated
- up_bias_grad: float32 [4304], replicated
All inputs are finite; a program needn't handle non-finite values.
Results may differ from a plain program's by a relative error of at most 0.018.
The roundings to bfloat16 on the way count: a program that leaves them out, or rounds other values in their place, can miss the bound.
Values may be sent and summed in bfloat16 or wider, within the bound.
A program may use at most 192 MiB of HBM per device.

v0:
```python
import math
import jax
import jax.numpy as jnp
from jax import lax
from jax.sharding import PartitionSpec as P

HD = 72
VALID = 729
norm_eps = 1e-06
gelu_coef = math.sqrt(2.0 / math.pi)


def norm_forward(values, scale_row, shift_row):
    average = jnp.mean(values, axis=-1, keepdims=True)
    centred = values - average
    inv_std = lax.rsqrt(jnp.mean(centred * centred, axis=-1, keepdims=True) + norm_eps)
    normed = centred * inv_std
    return (normed * scale_row + shift_row, normed, inv_std)


def norm_backward(upstream, normed, inv_std, scale_row):
    scaled = upstream * scale_row
    back = inv_std * (
        scaled
        - jnp.mean(scaled, axis=-1, keepdims=True)
        - normed * jnp.mean(scaled * normed, axis=-1, keepdims=True)
    )
    return (back, jnp.sum(upstream * normed, axis=0), jnp.sum(upstream, axis=0))


def gelu_tanh(pre_act):
    return (
        0.5
        * pre_act
        * (1.0 + jnp.tanh(gelu_coef * (pre_act + 0.044715 * pre_act * pre_act * pre_act)))
    )


def gelu_slope(pre_act):
    tangent = jnp.tanh(gelu_coef * (pre_act + 0.044715 * pre_act * pre_act * pre_act))
    inner_slope = gelu_coef * (1.0 + 3.0 * 0.044715 * pre_act * pre_act)
    return 0.5 * (1.0 + tangent) + 0.5 * pre_act * (1.0 - tangent * tangent) * inner_slope


def masked_scores(queries, key_rows, positions):
    seq_len = queries.shape[0]
    head_count = queries.shape[1] // HD
    query_heads = queries.reshape(seq_len, head_count, HD)
    key_heads = key_rows.reshape(seq_len, head_count, HD)
    scores = jnp.einsum("qhe,khe->hqk", query_heads, key_heads, preferred_element_type=jnp.float32)
    scores = scores * (1.0 / math.sqrt(HD))
    visible = (positions < VALID)[None, None, :]
    return (jnp.where(visible, scores, -1e30), query_heads, key_heads)


def attend_forward(queries, key_rows, values, positions):
    seq_len = queries.shape[0]
    scores, query_heads, key_heads = masked_scores(queries, key_rows, positions)
    value_heads = values.reshape(seq_len, -1, HD)
    largest = jnp.max(scores, axis=-1, keepdims=True)
    powers = jnp.exp(scores - largest)
    summed = jnp.sum(powers, axis=-1, keepdims=True)
    attn_probs = (powers / summed).astype(jnp.bfloat16)
    mixed_out = jnp.einsum(
        "hqk,khe->qhe", attn_probs, value_heads, preferred_element_type=jnp.float32
    )
    log_totals = (largest + jnp.log(summed))[:, :, 0]
    return (mixed_out.reshape(seq_len, queries.shape[1]).astype(jnp.bfloat16), log_totals)


def attend_backward(queries, key_rows, values, log_totals, d_mixed, positions):
    seq_len = queries.shape[0]
    scores, query_heads, key_heads = masked_scores(queries, key_rows, positions)
    value_heads = values.reshape(seq_len, -1, HD)
    grad_heads = d_mixed.reshape(seq_len, -1, HD)
    probs_full = jnp.exp(scores - log_totals[:, :, None])
    d_probs = jnp.einsum(
        "qhe,khe->hqk", grad_heads, value_heads, preferred_element_type=jnp.float32
    )
    row_inner = jnp.sum(probs_full * d_probs, axis=-1, keepdims=True)
    d_scores = (probs_full * (d_probs - row_inner)).astype(jnp.bfloat16)
    d_values = jnp.einsum(
        "hqk,qhe->khe",
        probs_full.astype(jnp.bfloat16),
        grad_heads,
        preferred_element_type=jnp.float32,
    )
    scale_now = 1.0 / math.sqrt(HD)
    d_queries = (
        jnp.einsum("hqk,khe->qhe", d_scores, key_heads, preferred_element_type=jnp.float32)
        * scale_now
    )
    d_keys = (
        jnp.einsum("hqk,qhe->khe", d_scores, query_heads, preferred_element_type=jnp.float32)
        * scale_now
    )
    parts = [d_queries, d_keys, d_values]
    return jnp.concatenate(
        [part.reshape(seq_len, queries.shape[1]).astype(jnp.bfloat16) for part in parts], axis=1
    )


def dot(left, right, dims):
    return lax.dot_general(left, right, (dims, ((), ())), preferred_element_type=jnp.float32)


ROWS_COLS = ((1,), (0,))
ROWS_ROWS = ((1,), (1,))
COLS_COLS = ((0,), (0,))


def swap_halves(block):
    return lax.ppermute(block, "tp", [(0, 1), (1, 0)])


def gather_rows(block):
    if lax.axis_size("tp") == 2:
        return jnp.concatenate([block, swap_halves(block)], axis=0)
    return lax.all_gather(block, "tp", axis=0, tiled=True)


def scatter_dot(left, right, dims):
    if lax.axis_size("tp") == 2:
        half = left.shape[0] // 2
        away = swap_halves(dot(left[half:], right, dims).astype(jnp.bfloat16))
        return dot(left[:half], right, dims) + away.astype(jnp.float32)
    return lax.psum_scatter(
        dot(left, right, dims).astype(jnp.bfloat16), "tp", scatter_dimension=0, tiled=True
    ).astype(jnp.float32)


def gather_weight(shard):
    return lax.all_gather(shard, "fsdp", axis=0, tiled=True)


def scatter_weight(whole):
    return lax.psum_scatter(
        whole.astype(jnp.bfloat16), "fsdp", scatter_dimension=0, tiled=False
    ).astype(jnp.float32)


def by_shard(whole):
    return whole.astype(jnp.bfloat16).reshape(lax.axis_size("fsdp"), -1, whole.shape[1])


def per_device(inputs, w_qkv, w_out, w_up, w_down, norm_gains, biases, up_bias, cotangent):
    image_count, rows_here, width = inputs.shape
    images = range(image_count)
    local_cols = w_qkv.shape[2]
    unit_count = w_up.shape[1]
    shard_rows = w_qkv.shape[1]
    tp_index = lax.axis_index("tp")
    seq_len = rows_here * lax.axis_size("tp")
    col_start = tp_index * local_cols
    unit_start = tp_index * unit_count
    positions = lax.iota(jnp.int32, seq_len)
    if lax.axis_size("tp") == 2:
        positions = positions + tp_index * rows_here
        positions = jnp.where(positions >= seq_len, positions - seq_len, positions)
    qkv_all = gather_weight(w_qkv.transpose(1, 0, 2).reshape(shard_rows, 3 * local_cols))
    out_all = gather_weight(w_out.T)
    up_all = gather_weight(w_up)
    down_all = gather_weight(w_down.T)
    query_bias = lax.dynamic_slice_in_dim(biases[1], col_start, local_cols)
    value_bias = lax.dynamic_slice_in_dim(biases[2], col_start, local_cols)
    unit_bias = lax.dynamic_slice_in_dim(up_bias, unit_start, unit_count)
    qkv_bias = jnp.concatenate([query_bias, jnp.zeros_like(query_bias), value_bias])
    residual = [inputs[i].astype(jnp.float32) for i in images]
    first = [norm_forward(residual[i], norm_gains[0], biases[0]) for i in images]
    gathered_one = [gather_rows(first[i][0].astype(jnp.bfloat16)) for i in images]
    grad_rows = [gather_rows(cotangent[i]) for i in images]
    saved, mixed, middle, second, gathered_two = ([], [], [], [], [])
    for i in images:
        projected = (dot(gathered_one[i], qkv_all, ROWS_COLS) + qkv_bias).astype(jnp.bfloat16)
        queries, key_rows, values = (
            projected[:, c * local_cols : (c + 1) * local_cols] for c in range(3)
        )
        mixed_out, log_totals = attend_forward(queries, key_rows, values, positions)
        saved.append((queries, key_rows, values, log_totals))
        mixed.append(mixed_out)
        middle.append(residual[i] + scatter_dot(mixed_out, out_all, ROWS_ROWS) + biases[3])
        second.append(norm_forward(middle[i], norm_gains[1], biases[4]))
        gathered_two.append(gather_rows(second[i][0].astype(jnp.bfloat16)))
    activated, d_pre, outputs, d_normed_two = ([], [], [], [])
    for i in images:
        pre_act = dot(gathered_two[i], up_all, ROWS_COLS) + unit_bias
        activated.append(gelu_tanh(pre_act).astype(jnp.bfloat16))
        d_act = dot(grad_rows[i], down_all, ROWS_COLS)
        d_pre.append((d_act * gelu_slope(pre_act)).astype(jnp.bfloat16))
        d_normed_two.append(scatter_dot(d_pre[i], up_all, ROWS_ROWS))
        mlp_rows = scatter_dot(activated[i], down_all, ROWS_ROWS)
        outputs.append((middle[i] + mlp_rows + biases[5]).astype(jnp.bfloat16))

    def joined(parts):
        return jnp.concatenate(parts, axis=0)

    grads_whole, units_whole = (joined(grad_rows), joined(d_pre))
    down_whole = by_shard(dot(grads_whole, joined(activated), COLS_COLS))
    up_whole = by_shard(dot(joined(gathered_two), units_whole, COLS_COLS))
    down_whole, up_whole, d_normed_two = lax.optimization_barrier(
        (down_whole, up_whole, d_normed_two)
    )
    down_grad = scatter_weight(down_whole).T
    up_grad = scatter_weight(up_whole)
    unit_sums = jnp.sum(units_whole, axis=0, dtype=jnp.float32)
    gain_two, shift_two, d_middle, branch = ([], [], [], [])
    for i in images:
        back, gain_part, shift_part = norm_backward(
            d_normed_two[i], second[i][1], second[i][2], norm_gains[1]
        )
        gain_two.append(gain_part)
        shift_two.append(shift_part)
        d_middle.append(cotangent[i].astype(jnp.float32) + back)
        branch.append(gather_rows(d_middle[i].astype(jnp.bfloat16)))
    d_qkv, d_normed_one = ([], [])
    for i in images:
        d_mixed = dot(branch[i], out_all, ROWS_COLS).astype(jnp.bfloat16)
        d_qkv.append(attend_backward(*saved[i], d_mixed, positions))
        d_normed_one.append(scatter_dot(d_qkv[i], qkv_all, ROWS_ROWS))
    out_grad = scatter_weight(by_shard(dot(joined(branch), joined(mixed), COLS_COLS))).T
    qkv_whole = joined(d_qkv)
    qkv_grad = scatter_weight(by_shard(dot(joined(gathered_one), qkv_whole, COLS_COLS)))
    qkv_grad = qkv_grad.reshape(shard_rows, 3, local_cols).transpose(1, 0, 2)
    qkv_sums = jnp.sum(qkv_whole, axis=0, dtype=jnp.float32)
    input_grad, gain_one, shift_one = ([], [], [])
    for i in images:
        back, gain_part, shift_part = norm_backward(
            d_normed_one[i], first[i][1], first[i][2], norm_gains[0]
        )
        gain_one.append(gain_part)
        shift_one.append(shift_part)
        input_grad.append(d_middle[i] + back)
    blank_row = jnp.zeros((width,), jnp.float32)
    query_sums = lax.dynamic_update_slice_in_dim(blank_row, qkv_sums[:local_cols], col_start, 0)
    value_sums = lax.dynamic_update_slice_in_dim(
        blank_row, qkv_sums[2 * local_cols :], col_start, 0
    )
    unit_row = lax.dynamic_update_slice_in_dim(jnp.zeros_like(up_bias), unit_sums, unit_start, 0)
    out_sums = sum((jnp.sum(d_middle[i], axis=0) for i in images))
    top_sums = jnp.sum(cotangent, axis=(0, 1), dtype=jnp.float32)
    pieces = [
        sum(gain_one),
        sum(shift_one),
        query_sums,
        value_sums,
        sum(gain_two),
        sum(shift_two),
        out_sums,
        top_sums,
        unit_row,
    ]
    total = lax.psum(jnp.concatenate(pieces), ("fsdp", "tp"))
    rows = total[: 8 * width].reshape(8, width)
    gain_total = jnp.stack([rows[0], rows[4]])
    bias_total = jnp.stack([rows[1], rows[2], rows[3], rows[6], rows[5], rows[7]])
    return (
        jnp.stack(outputs),
        jnp.stack(input_grad),
        qkv_grad,
        out_grad,
        up_grad,
        down_grad,
        gain_total,
        bias_total,
        total[8 * width :],
    )


def solution(mesh):
    return jax.shard_map(
        per_device,
        mesh=mesh,
        in_specs=(
            P("fsdp", "tp", None),
            P(None, "fsdp", "tp"),
            P("tp", "fsdp"),
            P("fsdp", "tp"),
            P("tp", "fsdp"),
            P(),
            P(),
            P(),
            P("fsdp", "tp", None),
        ),
        out_specs=(
            P("fsdp", "tp", None),
            P("fsdp", "tp", None),
            P(None, "fsdp", "tp"),
            P("tp", "fsdp"),
            P("fsdp", "tp"),
            P("tp", "fsdp"),
            P(),
            P(),
            P(),
        ),
        check_vma=False,
    )
```

profile of v0, /device:TPU:0, one launch (start us, length us, event | category | flops | bytes accessed | tf_op | source)
XLA Modules:
  0.0 743.1 jit_solution(5440039404475208873)
XLA Ops:
  16.4 3.0 collective-permute-start.4
  20.4 18.6 %collective-permute-done.4 = bf16[368,1152]{1,0:T(8,128)(2,1)S(1)} collective-permute-done((bf16[368,1152]{1,0:T(8,128)(2,1)S(1)}, bf16[368,1152]{1,0:T(8,128)(2,1)S(1)}, u32[]{:S(2)}, u32[]{:S(2)}) %collective-permute-start.4) | collective-permute-done | bytes 847904 | tf_op jit(solution)/shard_map/ppermute | solution.py:113
  39.0 24.9 %all-gather.5.cloned.1.call-done = bf16[1152,1728]{1,0:T(8,128)(2,1)} async-done(((bf16[72,1728]{1,0:T(8,128)(2,1)}), bf16[1152,1728]{1,0:T(8,128)(2,1)}) %all-gather.5.cloned.1.call-update) | async-done | bytes 3981328 | tf_op jit(solution)/shard_map/all_gather | solution.py:133
  63.9 6.5 add_convert_fusion
  75.1 2.6 copy.66
  77.7 6.3 add_convert_fusion.1
  84.1 2.0 fusion.199
  89.5 2.5 copy.62
  92.1 9.6 %fusion.204 = (f32[8,736]{1,0:T(8,128)}, f32[8,736,736]{1,2,0:T(8,128)}) fusion(bf16[736,8,72]{0,2,1:T(8,128)(2,1)S(1)} %bitcast.221, bf16[736,8,72]{0,2,1:T(8,128)(2,1)S(1)} %bitcast.211, pred[736]{0:T(1024)(128)(4,1)} %fusion.180), kind=kOutput, calls=%fused_computation.288 | convolution fusion | flops 637028608 | bytes 19054304 | tf_op jit(solution)/shard_map/qhe,khe->hqk/dot_general | solution.py:50
  101.7 9.4 %fusion = f32[8,736]{1,0:T(8,128)} fusion(f32[8,736,736]{1,2,0:T(8,128)} %get-tuple-element.110, f32[8,736]{1,0:T(8,128)} %get-tuple-element.109), kind=kLoop, calls=%fused_computation.12 | loop fusion | flops 8661248 | bytes 17381376 | tf_op jit(solution)/shard_map/reduce_sum | solution.py:62
  111.1 8.6 %fusion.157 = bf16[8,72,736]{2,1,0:T(8,128)(2,1)S(1)} fusion(bf16[736,8,72]{0,2,1:T(8,128)(2,1)S(1)} %bitcast.232, f32[8,736,736]{1,2,0:T(8,128)} %get-tuple-element.110, f32[8,736]{1,0:T(8,128)} %fusion, f32[8,736]{1,0:T(8,128)} %get-tuple-element.109), kind=kOutput, calls=%fused_computation.211 | convolution fusion | flops 637458432 | bytes 19077120 | tf_op jit(solution)/shard_map/hqk,khe->qhe/dot_general | solution.py:64
  120.8 3.2 convolution_convert_fusion.10
  125.5 9.2 %fusion.205 = (f32[8,736]{1,0:T(8,128)}, f32[8,736,736]{1,2,0:T(8,128)}) fusion(bf16[736,8,72]{0,2,1:T(8,128)(2,1)S(1)} %bitcast.223, bf16[736,8,72]{0,2,1:T(8,128)(2,1)S(1)} %bitcast.213, pred[736]{0:T(1024)(128)(4,1)S(1)} %copy-done.73), kind=kOutput, calls=%fused_computation.289 | convolution fusion | flops 637028608 | bytes 19054304 | tf_op jit(solution)/shard_map/qhe,khe->hqk/dot_general | solution.py:50
  134.7 8.8 %fusion.1 = f32[8,736]{1,0:T(8,128)S(1)} fusion(f32[8,736,736]{1,2,0:T(8,128)} %get-tuple-element.112, f32[8,736]{1,0:T(8,128)} %get-tuple-element.111), kind=kLoop, calls=%fused_computation.13 | loop fusion | flops 8661248 | bytes 17381376 | tf_op jit(solution)/shard_map/reduce_sum | solution.py:62
  143.5 8.8 %fusion.156 = bf16[8,72,736]{2,1,0:T(8,128)(2,1)S(1)} fusion(bf16[736,8,72]{0,2,1:T(8,128)(2,1)S(1)} %bitcast.234, f32[8,736,736]{1,2,0:T(8,128)} %get-tuple-element.112, f32[8,736]{1,0:T(8,128)S(1)} %fusion.1, f32[8,736]{1,0:T(8,128)S(1)} %copy-done.51), kind=kOutput, calls=%fused_computation.210 | convolution fusion | flops 637458432 | bytes 19077120 | tf_op jit(solution)/shard_map/hqk,khe->qhe/dot_general | solution.py:64
  154.8 19.7 %collective-permute-done.5 = bf16[368,1152]{1,0:T(8,128)(2,1)S(1)} collective-permute-done((bf16[368,1152]{1,0:T(8,128)(2,1)S(1)}, bf16[368,1152]{1,0:T(8,128)(2,1)S(1)}, u32[]{:S(2)}, u32[]{:S(2)}) %collective-permute-start.5) | collective-permute-done | bytes 847904 | tf_op jit(solution)/shard_map/ppermute | solution.py:113
  174.5 2.7 fusion.195
  185.2 16.6 %collective-permute-done.6 = bf16[368,1152]{1,0:T(8,128)(2,1)} collective-permute-done((bf16[368,1152]{1,0:T(8,128)(2,1)}, bf16[368,1152]{1,0:T(8,128)(2,1)}, u32[]{:S(2)}, u32[]{:S(2)}) %collective-permute-start.6) | collective-permute-done | bytes 847904 | tf_op jit(solution)/shard_map/ppermute | solution.py:113
  201.7 10.1 %fusion.112 = f32[736,2152]{1,0:T(8,128)} fusion(bf16[1152,2152]{1,0:T(8,128)(2,1)} %all-gather.9.cloned.1.call-done, bf16[368,1152]{1,0:T(8,128)(2,1)} %collective-permute-done.6, bf16[368,1152]{1,0:T(8,128)(2,1)} %get-tuple-element.102), kind=kOutput, calls=%fused_computation.155 | convolution fusion | flops 3652632576 | bytes 12989440 | tf_op jit(solution)/shard_map/dot_general | solution.py:104
  211.9 26.2 %collective-permute-done.9 = bf16[368,1152]{1,0:T(8,128)(2,1)} collective-permute-done((bf16[368,1152]{1,0:T(8,128)(2,1)}, bf16[368,1152]{1,0:T(8,128)(2,1)}, u32[]{:S(2)}, u32[]{:S(2)}) %collective-permute-start.9) | collective-permute-done | bytes 847904 | tf_op jit(solution)/shard_map/ppermute | solution.py:113
  238.1 11.2 %fusion.27 = bf16[736,2152]{1,0:T(8,128)(2,1)S(1)} fusion(bf16[1152,2152]{1,0:T(8,128)(2,1)} %all-gather.11.cloned.1.call-done, f32[736,2152]{1,0:T(8,128)} %fusion.112, f32[2152]{0:T(1024)S(1)} %dynamic_slice.17, bf16[368,1152]{1,0:T(8,128)(2,1)} %collective-permute-done.9, bf16[368,1152]{1,0:T(8,128)(2,1)} %get-tuple-element.86), kind=kOutput, calls=%fused_computation.46 | convolution fusion | flops 3684310016 | bytes 16165792 | tf_op jit(solution)/shard_map/dot_general | solution.py:104
  249.3 3.3 convolution_convert_fusion.5
  252.9 3.4 collective-permute-done.2
  256.2 11.5 %multiply_convert_fusion.3 = (bf16[736,2152]{1,0:T(8,128)(2,1)}, bf16[736,2152]{1,0:T(8,128)(2,1)}, f32[736,2152]{1,0:T(8,128)}) fusion(f32[2152]{0:T(1024)S(1)} %dynamic_slice.17, f32[736,2152]{1,0:T(8,128)} %fusion.112, bf16[1152,2152]{1,0:T(8,128)(2,1)S(1)} %copy-done.74, bf16[368,1152]{1,0:T(8,128)(2,1)} %collective-permute-done.2, ...), kind=kOutput, calls=%fused_computation.52 | convolution fusion | flops 3684310016 | bytes 25669024 | tf_op jit(solution)/shard_map/dot_general | solution.py:104
  267.7 9.5 %fusion.21 = bf16[736,2152]{1,0:T(8,128)(2,1)S(1)} fusion(bf16[1152,2152]{1,0:T(8,128)(2,1)S(1)} %bitcast.253, f32[736,2152]{1,0:T(8,128)} %get-tuple-element.113, f32[2152]{0:T(1024)S(1)} %dynamic_slice.17, bf16[368,1152]{1,0:T(8,128)(2,1)} %collective-permute-done.8, bf16[368,1152]{1,0:T(8,128)(2,1)} %get-tuple-element.85), kind=kOutput, calls=%fused_computation.40 | convolution fusion | flops 3684310016 | bytes 16165792 | tf_op jit(solution)/shard_map/dot_general | solution.py:104
  277.3 3.3 convolution_convert_fusion.6
  280.8 14.3 %convolution_convert_fusion = bf16[1152,2152]{0,1:T(8,128)(2,1)} fusion(bf16[736,2152]{1,0:T(8,128)(2,1)S(1)} %fusion.27, bf16[736,2152]{1,0:T(8,128)(2,1)S(1)} %fusion.21, bf16[368,1152]{1,0:T(8,128)(2,1)} %collective-permute-done.6, bf16[368,1152]{1,0:T(8,128)(2,1)} %get-tuple-element.102, bf16[368,1152]{1,0:T(8,128)(2,1)} %collective-permute-done.2, ...), kind=kOutput, calls=%fused_computation.17 | convolution fusion | flops 7327198208 | bytes 14685184 | tf_op jit(solution)/shard_map/dot_general | solution.py:104
  295.1 14.0 %convolution_convert_fusion.1 = bf16[1152,2152]{0,1:T(8,128)(2,1)} fusion(bf16[736,2152]{1,0:T(8,128)(2,1)S(1)} %copy-done.83, bf16[736,2152]{1,0:T(8,128)(2,1)S(1)} %copy-done.80, bf16[368,1152]{1,0:T(8,128)(2,1)} %collective-permute-done.9, bf16[368,1152]{1,0:T(8,128)(2,1)} %get-tuple-element.86, bf16[368,1152]{1,0:T(8,128)(2,1)} %collective-permute-done.8, ...), kind=kOutput, calls=%fused_computation.18 | convolution fusion | flops 7327198208 | bytes 14685184 | tf_op jit(solution)/shard_map/dot_general | solution.py:104
  309.1 8.4 %copy.71 = bf16[1152,2152]{1,0:T(8,128)(2,1)} copy(bf16[1152,2152]{0,1:T(8,128)(2,1)} %convolution_convert_fusion) | data formatting | bytes 9916416 | tf_op jit(solution)/shard_map/convert_element_type | solution.py:143
  317.5 8.8 %copy.70 = bf16[1152,2152]{1,0:T(8,128)(2,1)} copy(bf16[1152,2152]{0,1:T(8,128)(2,1)} %convolution_convert_fusion.1) | data formatting | bytes 9916416 | tf_op jit(solution)/shard_map/convert_element_type | solution.py:143
  326.3 6.9 convert_add_fusion.2
  333.1 6.2 convert_add_fusion.3
  339.4 4.1 multiply_reduce_fusion.3
  343.5 2.1 fusion.194
  348.0 19.6 %collective-permute-done.14 = bf16[368,1152]{1,0:T(8,128)(2,1)S(1)} collective-permute-done((bf16[368,1152]{1,0:T(8,128)(2,1)S(1)}, bf16[368,1152]{1,0:T(8,128)(2,1)S(1)}, u32[]{:S(2)}, u32[]{:S(2)}) %collective-permute-start.14) | collective-permute-done | bytes 847904 | tf_op jit(solution)/shard_map/ppermute | solution.py:113
  369.0 11.6 %multiply_reduce_fusion = (f32[8,736]{1,0:T(8,128)S(1)}, f32[8,736,736]{1,2,0:T(8,128)}) fusion(f32[8,736,736]{1,2,0:T(8,128)} %get-tuple-element.112, f32[8,736]{1,0:T(8,128)S(1)} %log_add_fusion, bf16[736,8,72]{0,2,1:T(8,128)(2,1)S(1)} %bitcast.236, bf16[736,8,72]{0,2,1:T(8,128)(2,1)S(1)} %bitcast.235), kind=kOutput, calls=%fused_computation.1 | convolution fusion | flops 637028608 | bytes 36411392 | tf_op jit(solution)/shard_map/qhe,khe->hqk/dot_general | solution.py:77
  380.6 12.7 %multiply_convert_fusion = bf16[8,736,736]{1,2,0:T(8,128)(2,1)S(1)} fusion(f32[8,736,736]{1,2,0:T(8,128)} %get-tuple-element.117, f32[8,736,736]{1,2,0:T(8,128)} %get-tuple-element.112, f32[8,736]{1,0:T(8,128)S(1)} %get-tuple-element.116, f32[8,736]{1,0:T(8,128)S(1)} %log_add_fusion), kind=kLoop, calls=%fused_computation | loop fusion | flops 17334272 | bytes 43382784 | tf_op jit(solution)/shard_map/convert_element_type | solution.py:81
  393.3 3.7 multiply_convert_fusion.4
  397.0 2.6 multiply_convert_fusion.5
  399.6 9.9 %fusion.161 = bf16[8,72,736]{2,1,0:T(8,128)(2,1)} fusion(bf16[736,8,72]{0,2,1:T(8,128)(2,1)S(1)} %bitcast.237, f32[8,736,736]{1,2,0:T(8,128)} %get-tuple-element.112, f32[8,736]{1,0:T(8,128)S(1)} %log_add_fusion), kind=kOutput, calls=%fused_computation.213 | convolution fusion | flops 633124864 | bytes 19053568 | tf_op jit(solution)/shard_map/hqk,qhe->khe/dot_general | solution.py:82
  410.9 9.9 %fusion.158 = bf16[8,72,736]{2,1,0:T(8,128)(2,1)} fusion(bf16[736,8,72]{0,2,1:T(8,128)(2,1)S(1)} %bitcast.238, f32[8,736,736]{1,2,0:T(8,128)} %get-tuple-element.110, f32[8,736]{1,0:T(8,128)S(1)} %log_add_fusion.1), kind=kOutput, calls=%fused_computation.212 | convolution fusion | flops 633124864 | bytes 19053568 | tf_op jit(solution)/shard_map/hqk,qhe->khe/dot_general | solution.py:82
  420.9 12.0 %multiply_reduce_fusion.1 = (f32[8,736]{1,0:T(8,128)S(1)}, f32[8,736,736]{1,2,0:T(8,128)}) fusion(f32[8,736,736]{1,2,0:T(8,128)} %get-tuple-element.110, f32[8,736]{1,0:T(8,128)S(1)} %log_add_fusion.1, bf16[736,8,72]{0,2,1:T(8,128)(2,1)S(1)} %bitcast.239, bf16[736,8,72]{0,2,1:T(8,128)(2,1)S(1)} %bitcast.233), kind=kOutput, calls=%fused_computation.4 | convolution fusion | flops 637028608 | bytes 36411392 | tf_op jit(solution)/shard_map/qhe,khe->hqk/dot_general | solution.py:77
  432.9 3.6 fusion.60
  436.5 2.6 copy.79
  439.2 13.1 %multiply_convert_fusion.1 = bf16[8,736,736]{1,2,0:T(8,128)(2,1)S(1)} fusion(f32[8,736,736]{1,2,0:T(8,128)} %get-tuple-element.115, f32[8,736,736]{1,2,0:T(8,128)} %get-tuple-element.110, f32[8,736]{1,0:T(8,128)S(1)} %get-tuple-element.114, f32[8,736]{1,0:T(8,128)S(1)} %log_add_fusion.1), kind=kLoop, calls=%fused_computation.3 | loop fusion | flops 17334272 | bytes 43382784 | tf_op jit(solution)/shard_map/convert_element_type | solution.py:81
  452.3 2.8 multiply_convert_fusion.6
  458.5 10.3 %convolution_convert_fusion.2 = bf16[1152,1728]{0,1:T(8,128)(2,1)} fusion(bf16[368,1152]{1,0:T(8,128)(2,1)S(1)} %copy-done.77, bf16[368,1152]{1,0:T(8,128)(2,1)S(1)} %copy-done.49, bf16[368,1152]{1,0:T(8,128)(2,1)S(1)} %copy-done.79, bf16[368,1152]{1,0:T(8,128)(2,1)} %get-tuple-element.77, bf16[736,576]{0,1:T(8,128)(2,1)S(1)} %bitcast.225, ...), kind=kOutput, calls=%fused_computation.30 | convolution fusion | flops 5906571264 | bytes 12460032 | tf_op jit(solution)/shard_map/dot_general | solution.py:104
  468.8 6.4 copy.78
  478.0 6.3 convolution_convert_fusion.7
  485.8 6.1 convolution_convert_fusion.9
  493.8 11.8 %collective-permute-done.7 = bf16[368,1152]{1,0:T(8,128)(2,1)} collective-permute-done((bf16[368,1152]{1,0:T(8,128)(2,1)}, bf16[368,1152]{1,0:T(8,128)(2,1)}, u32[]{:S(2)}, u32[]{:S(2)}) %collective-permute-start.7) | collective-permute-done | bytes 847904 | tf_op jit(solution)/shard_map/ppermute | solution.py:113
  505.7 6.2 fusion.145
  511.8 2.9 collective-permute-done.3
  514.7 5.3 fusion.153
  526.3 2.5 convolution_convert_fusion.3
  530.6 2.5 convolution_convert_fusion.4
  533.4 23.4 %convert_reduce_fusion.1 = f32[1728]{0:T(1024)S(1)} fusion(bf16[736,576]{0,1:T(8,128)(2,1)S(1)} %bitcast.227, bf16[736,576]{0,1:T(8,128)(2,1)S(1)} %bitcast.217, bf16[736,576]{0,1:T(8,128)(2,1)S(1)} %bitcast.207, bf16[736,576]{0,1:T(8,128)(2,1)S(1)} %bitcast.230, bf16[736,576]{0,1:T(8,128)(2,1)S(1)} %bitcast.220, bf16[736,576]{0,1:T(8,128)(2,1)S(1)} %bitcast.210), kind=kLoop, calls=%fused_computation.19 | loop fusion | flops 33065280 | bytes 5094144 | tf_op jit(solution)/shard_map/reduce_sum | solution.py:224
  557.3 2.0 convert_add_fusion
  559.5 4.3 fusion.98
  564.0 39.7 %psum.7 = f32[13520]{0:T(1024)S(1)} all-reduce(f32[13520]{0:T(1024)S(1)} %constant_dynamic-update-slice_fusion), channel_id=1, replica_groups=mesh['fsdp'=16,'tp'=2] {'fsdp','tp'}, use_global_device_ids=true, to_apply=%region_39.40 | all-reduce | flops 13520 | bytes 108160 | tf_op jit(solution)/shard_map/psum | solution.py:252
  605.7 3.1 fusion.97
  608.8 2.0 pad_maximum_fusion.2
  614.4 38.4 %reduce-scatter.17.cloned.1.call-done = bf16[1,72,2152]{2,1,0:T(8,128)(2,1)} async-done(((bf16[16,72,2152]{2,1,0:T(8,128)(2,1)}), bf16[1,72,2152]{2,1,0:T(8,128)(2,1)}) %reduce-scatter.17.cloned.1.call-update) | async-done | bytes 309904
  654.6 79.5 %reduce-scatter.15.cloned.1.call-done = bf16[1,72,2152]{2,1,0:T(8,128)(2,1)} async-done(((bf16[16,72,2152]{2,1,0:T(8,128)(2,1)}), bf16[1,72,2152]{2,1,0:T(8,128)(2,1)}) %reduce-scatter.15.cloned.1.call-update) | async-done | bytes 309904
  (302 shorter events, 64.6 us)
Async XLA Ops:
  7.2 7.0 copy-start.66
  7.2 56.7 %all-gather.5.cloned.1.call-start = ((), (), s32[]{:S(2)}) async-start(), calls=%async_computation.4 | async-start | bytes 4386816 | tf_op jit(solution)/shard_map/all_gather | solution.py:133
  9.4 111.3 %all-gather.7.cloned.1.call-start = ((), (), s32[]{:S(2)}) async-start(), calls=%async_computation.5 | async-start | bytes 1566720 | tf_op jit(solution)/shard_map/all_gather | solution.py:133
  10.2 191.6 %all-gather.9.cloned.1.call-start = ((), (), s32[]{:S(2)}) async-start(), calls=%async_computation.6 | async-start | bytes 5326848 | tf_op jit(solution)/shard_map/all_gather | solution.py:133
  10.9 227.2 %all-gather.11.cloned.1.call-start = ((), (), s32[]{:S(2)}) async-start(), calls=%async_computation.7 | async-start | bytes 5326848 | tf_op jit(solution)/shard_map/all_gather | solution.py:133
  13.5 50.4 %copy-start.59 = (f32[368]{0:T(512)}, f32[368]{0:T(512)S(1)}, u32[]{:S(2)}) copy-start(f32[368]{0:T(512)S(1)} %get-tuple-element.121) | copy-start | bytes 4420
  13.5 50.4 %copy-start.61 = (f32[368]{0:T(512)}, f32[368]{0:T(512)S(1)}, u32[]{:S(2)}) copy-start(f32[368]{0:T(512)S(1)} %get-tuple-element.122) | copy-start | bytes 4420
  14.1 49.8 %copy-start.67 = (f32[368]{0:T(512)}, f32[368]{0:T(512)S(1)}, u32[]{:S(2)}) copy-start(f32[368]{0:T(512)S(1)} %add_rsqrt_fusion.3) | copy-start | bytes 4420
  14.2 49.7 %copy-start.69 = (f32[368]{0:T(512)}, f32[368]{0:T(512)S(1)}, u32[]{:S(2)}) copy-start(f32[368]{0:T(512)S(1)} %add_rsqrt_fusion.1) | copy-start | bytes 4420
  16.4 47.5 %copy-start.48 = (bf16[368,1152]{1,0:T(8,128)(2,1)}, bf16[368,1152]{1,0:T(8,128)(2,1)S(1)}, u32[]{:S(2)}) copy-start(bf16[368,1152]{1,0:T(8,128)(2,1)S(1)} %get-tuple-element.78) | copy-start | bytes 2543620
  16.4 22.7 %collective-permute-start.4 = (bf16[368,1152]{1,0:T(8,128)(2,1)S(1)}, bf16[368,1152]{1,0:T(8,128)(2,1)S(1)}, u32[]{:S(2)}, u32[]{:S(2)}) collective-permute-start(bf16[368,1152]{1,0:T(8,128)(2,1)S(1)} %get-tuple-element.78), channel_id=1, source_target_pairs={{0,1},{1,0},{2,3},{3,2},{4,5},{5,4},{6,7},{7,6},{8,9},{9,8},{10,11... | collective-permute-start | bytes 2543624 | tf_op jit(solution)/shard_map/ppermute | solution.py:113
  19.4 58.4 %collective-permute-start = (bf16[368,1152]{1,0:T(8,128)(2,1)}, bf16[368,1152]{1,0:T(8,128)(2,1)S(1)}, u32[]{:S(2)}, u32[]{:S(2)}) collective-permute-start(bf16[368,1152]{1,0:T(8,128)(2,1)} %get-tuple-element.77), channel_id=1, source_target_pairs={{0,1},{1,0},{2,3},{3,2},{4,5},{5,4},{6,7},{7,6},{8,9},{9,8},{10,11... | collective-permute-start | bytes 2543624 | tf_op jit(solution)/shard_map/ppermute | solution.py:113
  19.4 591.3 %reduce-scatter.13.cloned.1.call-start = ((), (), s32[]{:S(2)}) async-start(), calls=%async_computation.9 | async-start | bytes 1566720
  39.0 24.9 %copy-start.76 = (bf16[368,1152]{1,0:T(8,128)(2,1)}, bf16[368,1152]{1,0:T(8,128)(2,1)S(1)}, u32[]{:S(2)}) copy-start(bf16[368,1152]{1,0:T(8,128)(2,1)S(1)} %collective-permute-done.4) | copy-start | bytes 2543620
  73.3 52.2 %copy-start.14 = (bf16[736,576]{0,1:T(8,128)(2,1)}, bf16[736,576]{0,1:T(8,128)(2,1)S(1)}, u32[]{:S(2)}) copy-start(bf16[736,576]{0,1:T(8,128)(2,1)S(1)} %copy.68) | copy-start | bytes 2543620
  75.1 50.3 %copy-start.22 = (bf16[736,576]{0,1:T(8,128)(2,1)}, bf16[736,576]{0,1:T(8,128)(2,1)S(1)}, u32[]{:S(2)}) copy-start(bf16[736,576]{0,1:T(8,128)(2,1)S(1)} %copy.67) | copy-start | bytes 2543620
  87.6 14.1 %copy-start.12 = (bf16[736,576]{0,1:T(8,128)(2,1)}, bf16[736,576]{0,1:T(8,128)(2,1)S(1)}, u32[]{:S(2)}) copy-start(bf16[736,576]{0,1:T(8,128)(2,1)S(1)} %copy.64) | copy-start | bytes 2543620
  89.5 12.2 %copy-start.20 = (bf16[736,576]{0,1:T(8,128)(2,1)}, bf16[736,576]{0,1:T(8,128)(2,1)S(1)}, u32[]{:S(2)}) copy-start(bf16[736,576]{0,1:T(8,128)(2,1)S(1)} %copy.63) | copy-start | bytes 2543620
  101.7 9.4 %copy-start.32 = (bf16[736,576]{0,1:T(8,128)(2,1)S(1)}, bf16[736,576]{0,1:T(8,128)(2,1)}, u32[]{:S(2)}) copy-start(bf16[736,576]{0,1:T(8,128)(2,1)} %copy.62) | copy-start | bytes 2543620
  119.7 15.0 %copy-start.43 = (bf16[8,72,736]{2,1,0:T(8,128)(2,1)}, bf16[8,72,736]{2,1,0:T(8,128)(2,1)S(1)}, u32[]{:S(2)}) copy-start(bf16[8,72,736]{2,1,0:T(8,128)(2,1)S(1)} %fusion.157) | copy-start | bytes 2543620
  124.0 30.8 %collective-permute-start.1 = (bf16[368,1152]{1,0:T(8,128)(2,1)}, bf16[368,1152]{1,0:T(8,128)(2,1)}, u32[]{:S(2)}, u32[]{:S(2)}) collective-permute-start(bf16[368,1152]{1,0:T(8,128)(2,1)} %convolution_convert_fusion.10), channel_id=1, source_target_pairs={{0,1},{1,0},{2,3},{3,2},{4,5},{5,4},{6,7},{7,6},{8,9},{9,8},{10,11... | collective-permute-start | bytes 2543624 | tf_op jit(solution)/shard_map/ppermute | solution.py:113
  134.7 8.8 %copy-start.34 = (bf16[736,576]{0,1:T(8,128)(2,1)S(1)}, bf16[736,576]{0,1:T(8,128)(2,1)}, u32[]{:S(2)}) copy-start(bf16[736,576]{0,1:T(8,128)(2,1)} %copy.66) | copy-start | bytes 2543620
  134.7 8.8 %copy-start.51 = (f32[8,736]{1,0:T(8,128)S(1)}, f32[8,736]{1,0:T(8,128)}, u32[]{:S(2)}) copy-start(f32[8,736]{1,0:T(8,128)} %get-tuple-element.111) | copy-start | bytes 70660
  143.5 9.1 %copy-start.30 = (bf16[1152,576]{1,0:T(8,128)(2,1)S(1)}, bf16[1152,576]{1,0:T(8,128)(2,1)}, u32[]{:S(2)}) copy-start(bf16[1152,576]{1,0:T(8,128)(2,1)} %all-gather.7.cloned.1.call-done) | copy-start | bytes 3981316
  152.5 21.9 %copy-start.1 = (bf16[2,368,1152]{2,1,0:T(8,128)(2,1)S(1)}, bf16[2,368,1152]{2,1,0:T(8,128)(2,1)}, u32[]{:S(2)}) copy-start(bf16[2,368,1152]{2,1,0:T(8,128)(2,1)} %param.9) | copy-start | bytes 5087236
  152.6 21.9 %copy-start.41 = (bf16[368,8,72]{0,2,1:T(8,128)(2,1)S(1)}, bf16[368,8,72]{0,2,1:T(8,128)(2,1)}, u32[]{:S(2)}) copy-start(bf16[368,8,72]{0,2,1:T(8,128)(2,1)} %get-tuple-element.88) | copy-start | bytes 1271812
  152.6 21.9 %copy-start.65 = (f32[1152]{0:T(1024)S(1)}, f32[1152]{0:T(1024)}, u32[]{:S(2)}) copy-start(f32[1152]{0:T(1024)} %get-tuple-element.58) | copy-start | bytes 13828
  153.6 20.9 %collective-permute-start.5 = (bf16[368,1152]{1,0:T(8,128)(2,1)S(1)}, bf16[368,1152]{1,0:T(8,128)(2,1)S(1)}, u32[]{:S(2)}, u32[]{:S(2)}) collective-permute-start(bf16[368,1152]{1,0:T(8,128)(2,1)S(1)} %convolution_convert_fusion.8), channel_id=1, source_target_pairs={{0,1},{1,0},{2,3},{3,2},{4,5},{5,4},{6,7},{7,6},{8,9},{9,8},{10,11... | collective-permute-start | bytes 2543624 | tf_op jit(solution)/shard_map/ppermute | solution.py:113
  179.6 22.1 %collective-permute-start.6 = (bf16[368,1152]{1,0:T(8,128)(2,1)}, bf16[368,1152]{1,0:T(8,128)(2,1)}, u32[]{:S(2)}, u32[]{:S(2)}) collective-permute-start(bf16[368,1152]{1,0:T(8,128)(2,1)} %get-tuple-element.102), channel_id=1, source_target_pairs={{0,1},{1,0},{2,3},{3,2},{4,5},{5,4},{6,7},{7,6},{8,9},{9,8},{10,11... | collective-permute-start | bytes 2543624 | tf_op jit(solution)/shard_map/ppermute | solution.py:113
  181.3 86.4 %collective-permute-start.8 = (bf16[368,1152]{1,0:T(8,128)(2,1)}, bf16[368,1152]{1,0:T(8,128)(2,1)}, u32[]{:S(2)}, u32[]{:S(2)}) collective-permute-start(bf16[368,1152]{1,0:T(8,128)(2,1)} %get-tuple-element.85), channel_id=1, source_target_pairs={{0,1},{1,0},{2,3},{3,2},{4,5},{5,4},{6,7},{7,6},{8,9},{9,8},{10,11... | collective-permute-start | bytes 2543624 | tf_op jit(solution)/shard_map/ppermute | solution.py:113
  183.0 55.0 %collective-permute-start.9 = (bf16[368,1152]{1,0:T(8,128)(2,1)}, bf16[368,1152]{1,0:T(8,128)(2,1)}, u32[]{:S(2)}, u32[]{:S(2)}) collective-permute-start(bf16[368,1152]{1,0:T(8,128)(2,1)} %get-tuple-element.86), channel_id=1, source_target_pairs={{0,1},{1,0},{2,3},{3,2},{4,5},{5,4},{6,7},{7,6},{8,9},{9,8},{10,11... | collective-permute-start | bytes 2543624 | tf_op jit(solution)/shard_map/ppermute | solution.py:113
  183.4 72.8 %collective-permute-start.2 = (bf16[368,1152]{1,0:T(8,128)(2,1)}, bf16[368,1152]{1,0:T(8,128)(2,1)}, u32[]{:S(2)}, u32[]{:S(2)}) collective-permute-start(bf16[368,1152]{1,0:T(8,128)(2,1)} %get-tuple-element.101), channel_id=1, source_target_pairs={{0,1},{1,0},{2,3},{3,2},{4,5},{5,4},{6,7},{7,6},{8,9},{9,8},{10,11... | collective-permute-start | bytes 2543624 | tf_op jit(solution)/shard_map/ppermute | solution.py:113
  238.1 11.2 %copy-start.74 = (bf16[1152,2152]{1,0:T(8,128)(2,1)S(1)}, bf16[1152,2152]{1,0:T(8,128)(2,1)}, u32[]{:S(2)}) copy-start(bf16[1152,2152]{1,0:T(8,128)(2,1)} %all-gather.9.cloned.1.call-done) | copy-start | bytes 14874628
  249.3 31.5 %copy-start.36 = (bf16[736,2152]{1,0:T(8,128)(2,1)}, bf16[736,2152]{1,0:T(8,128)(2,1)S(1)}, u32[]{:S(2)}) copy-start(bf16[736,2152]{1,0:T(8,128)(2,1)S(1)} %fusion.27) | copy-start | bytes 9503236
  249.3 18.4 %slice-start = ((s8[5013504]{0:T(1024)(128)(4,1)}), s8[4194304]{0:T(1024)(128)(4,1)S(1)}, s32[]{:S(2)}) async-start(s8[5013504]{0:T(1024)(128)(4,1)} %bitcast.252), calls=%async_computation.12 | async-start | bytes 8388608
  252.6 15.1 %slice-start.1 = ((s8[5013504]{0:T(1024)(128)(4,1)}), s8[819200]{0:T(1024)(128)(4,1)S(1)}, s32[]{:S(2)}) async-start(s8[5013504]{0:T(1024)(128)(4,1)} %bitcast.252), calls=%async_computation.13 | async-start | bytes 1638400
  252.6 73.7 %collective-permute-start.11 = (bf16[368,1152]{1,0:T(8,128)(2,1)}, bf16[368,1152]{1,0:T(8,128)(2,1)}, u32[]{:S(2)}, u32[]{:S(2)}) collective-permute-start(bf16[368,1152]{1,0:T(8,128)(2,1)} %convolution_convert_fusion.5), channel_id=1, source_target_pairs={{0,1},{1,0},{2,3},{3,2},{4,5},{5,4},{6,7},{7,6},{8,9},{9,8},{10,11... | collective-permute-start | bytes 2543624 | tf_op jit(solution)/shard_map/ppermute | solution.py:113
  280.5 14.6 %copy-start.80 = (bf16[736,2152]{1,0:T(8,128)(2,1)S(1)}, bf16[736,2152]{1,0:T(8,128)(2,1)}, u32[]{:S(2)}) copy-start(bf16[736,2152]{1,0:T(8,128)(2,1)} %get-tuple-element.103) | copy-start | bytes 9503236
  280.5 14.6 %copy-start.83 = (bf16[736,2152]{1,0:T(8,128)(2,1)S(1)}, bf16[736,2152]{1,0:T(8,128)(2,1)}, u32[]{:S(2)}) copy-start(bf16[736,2152]{1,0:T(8,128)(2,1)} %get-tuple-element.104) | copy-start | bytes 9503236
  280.5 52.6 %collective-permute-start.10 = (bf16[368,1152]{1,0:T(8,128)(2,1)}, bf16[368,1152]{1,0:T(8,128)(2,1)}, u32[]{:S(2)}, u32[]{:S(2)}) collective-permute-start(bf16[368,1152]{1,0:T(8,128)(2,1)} %convolution_convert_fusion.6), channel_id=1, source_target_pairs={{0,1},{1,0},{2,3},{3,2},{4,5},{5,4},{6,7},{7,6},{8,9},{9,8},{10,11... | collective-permute-start | bytes 2543624 | tf_op jit(solution)/shard_map/ppermute | solution.py:113
  345.6 23.4 %copy-start.5 = (f32[368,1152]{1,0:T(8,128)}, f32[368,1152]{1,0:T(8,128)S(1)}, u32[]{:S(2)}) copy-start(f32[368,1152]{1,0:T(8,128)S(1)} %get-tuple-element.66) | copy-start | bytes 5087236
  345.6 23.4 %copy-start.7 = (f32[368,1152]{1,0:T(8,128)}, f32[368,1152]{1,0:T(8,128)S(1)}, u32[]{:S(2)}) copy-start(f32[368,1152]{1,0:T(8,128)S(1)} %get-tuple-element.82) | copy-start | bytes 5087236
  345.6 22.0 %copy-start.31 = (bf16[1152,576]{1,0:T(8,128)(2,1)S(1)}, bf16[1152,576]{1,0:T(8,128)(2,1)}, u32[]{:S(2)}) copy-start(bf16[1152,576]{1,0:T(8,128)(2,1)} %all-gather.7.cloned.1.call-done) | copy-start | bytes 3981316
  345.7 21.9 %collective-permute-start.14 = (bf16[368,1152]{1,0:T(8,128)(2,1)S(1)}, bf16[368,1152]{1,0:T(8,128)(2,1)S(1)}, u32[]{:S(2)}, u32[]{:S(2)}) collective-permute-start(bf16[368,1152]{1,0:T(8,128)(2,1)S(1)} %convert_element_type.297), channel_id=1, source_target_pairs={{0,1},{1,0},{2,3},{3,2},{4,5},{5,4},{6,7},{7,6},{8,9},{9,8},{10,11... | collective-permute-start | bytes 2543624 | tf_op jit(solution)/shard_map/ppermute | solution.py:113
  347.4 21.6 %copy-start.35 = (bf16[736,576]{0,1:T(8,128)(2,1)S(1)}, bf16[736,576]{0,1:T(8,128)(2,1)}, u32[]{:S(2)}) copy-start(bf16[736,576]{0,1:T(8,128)(2,1)} %copy.66) | copy-start | bytes 2543620
  347.4 62.1 %collective-permute-start.12 = (bf16[368,1152]{1,0:T(8,128)(2,1)S(1)}, bf16[368,1152]{1,0:T(8,128)(2,1)S(1)}, u32[]{:S(2)}, u32[]{:S(2)}) collective-permute-start(bf16[368,1152]{1,0:T(8,128)(2,1)S(1)} %convert_element_type.281), channel_id=1, source_target_pairs={{0,1},{1,0},{2,3},{3,2},{4,5},{5,4},{6,7},{7,6},{8,9},{9,8},{10,11... | collective-permute-start | bytes 2543624 | tf_op jit(solution)/shard_map/ppermute | solution.py:113
  380.6 12.7 %copy-start.23 = (bf16[736,576]{0,1:T(8,128)(2,1)S(1)}, bf16[736,576]{0,1:T(8,128)(2,1)}, u32[]{:S(2)}) copy-start(bf16[736,576]{0,1:T(8,128)(2,1)} %copy-done.22) | copy-start | bytes 2543620
  410.9 10.0 %copy-start.33 = (bf16[736,576]{0,1:T(8,128)(2,1)S(1)}, bf16[736,576]{0,1:T(8,128)(2,1)}, u32[]{:S(2)}) copy-start(bf16[736,576]{0,1:T(8,128)(2,1)} %copy.62) | copy-start | bytes 2543620
  420.9 12.0 %copy-start.44 = (bf16[8,72,736]{2,1,0:T(8,128)(2,1)S(1)}, bf16[8,72,736]{2,1,0:T(8,128)(2,1)}, u32[]{:S(2)}) copy-start(bf16[8,72,736]{2,1,0:T(8,128)(2,1)} %copy-done.43) | copy-start | bytes 2543620
  420.9 12.0 %copy-start.46 = (bf16[8,72,736]{2,1,0:T(8,128)(2,1)S(1)}, bf16[8,72,736]{2,1,0:T(8,128)(2,1)}, u32[]{:S(2)}) copy-start(bf16[8,72,736]{2,1,0:T(8,128)(2,1)} %copy-done.45) | copy-start | bytes 2543620
  439.2 173.1 %reduce-scatter.11.cloned.1.call-start = ((), (), s32[]{:S(2)}) async-start(), calls=%async_computation.8 | async-start | bytes 4386816 | tf_op jit(solution)/shard_map/reduce_scatter | solution.py:137
  439.2 13.1 %copy-start.21 = (bf16[736,576]{0,1:T(8,128)(2,1)S(1)}, bf16[736,576]{0,1:T(8,128)(2,1)}, u32[]{:S(2)}) copy-start(bf16[736,576]{0,1:T(8,128)(2,1)} %copy-done.20) | copy-start | bytes 2543620
  475.3 177.5 %reduce-scatter.17.cloned.1.call-start = ((), (), s32[]{:S(2)}) async-start(), calls=%async_computation.11 | async-start | bytes 5326848
  476.0 258.2 %reduce-scatter.15.cloned.1.call-start = ((), (), s32[]{:S(2)}) async-start(), calls=%async_computation.10 | async-start | bytes 5326848
  478.0 7.8 %copy-start.81 = (bf16[736,2152]{1,0:T(8,128)(2,1)S(1)}, bf16[736,2152]{1,0:T(8,128)(2,1)}, u32[]{:S(2)}) copy-start(bf16[736,2152]{1,0:T(8,128)(2,1)} %get-tuple-element.103) | copy-start | bytes 9503236
  484.4 8.1 %copy-start.37 = (bf16[736,2152]{1,0:T(8,128)(2,1)S(1)}, bf16[736,2152]{1,0:T(8,128)(2,1)}, u32[]{:S(2)}) copy-start(bf16[736,2152]{1,0:T(8,128)(2,1)} %copy-done.36) | copy-start | bytes 9503236
  484.4 8.1 %copy-start.40 = (bf16[736,2152]{1,0:T(8,128)(2,1)S(1)}, bf16[736,2152]{1,0:T(8,128)(2,1)}, u32[]{:S(2)}) copy-start(bf16[736,2152]{1,0:T(8,128)(2,1)} %copy-done.38) | copy-start | bytes 9503236
  484.4 21.3 %collective-permute-start.7 = (bf16[368,1152]{1,0:T(8,128)(2,1)}, bf16[368,1152]{1,0:T(8,128)(2,1)}, u32[]{:S(2)}, u32[]{:S(2)}) collective-permute-start(bf16[368,1152]{1,0:T(8,128)(2,1)} %convolution_convert_fusion.7), channel_id=1, source_target_pairs={{0,1},{1,0},{2,3},{3,2},{4,5},{5,4},{6,7},{7,6},{8,9},{9,8},{10,11... | collective-permute-start | bytes 2543624 | tf_op jit(solution)/shard_map/ppermute | solution.py:113
  492.0 13.7 %copy-start.71 = (f32[1152]{0:T(1024)S(1)}, f32[1152]{0:T(1024)}, u32[]{:S(2)}) copy-start(f32[1152]{0:T(1024)} %get-tuple-element.57) | copy-start | bytes 13828
  492.0 22.8 %collective-permute-start.3 = (bf16[368,1152]{1,0:T(8,128)(2,1)}, bf16[368,1152]{1,0:T(8,128)(2,1)}, u32[]{:S(2)}, u32[]{:S(2)}) collective-permute-start(bf16[368,1152]{1,0:T(8,128)(2,1)} %convolution_convert_fusion.9), channel_id=1, source_target_pairs={{0,1},{1,0},{2,3},{3,2},{4,5},{5,4},{6,7},{7,6},{8,9},{9,8},{10,11... | collective-permute-start | bytes 2543624 | tf_op jit(solution)/shard_map/ppermute | solution.py:113
  505.6 9.1 %copy-start.82 = (bf16[736,2152]{1,0:T(8,128)(2,1)S(1)}, bf16[736,2152]{1,0:T(8,128)(2,1)}, u32[]{:S(2)}) copy-start(bf16[736,2152]{1,0:T(8,128)(2,1)} %get-tuple-element.103) | copy-start | bytes 9503236
  528.7 28.6 %collective-permute-start.15 = (bf16[368,1152]{1,0:T(8,128)(2,1)S(1)}, bf16[368,1152]{1,0:T(8,128)(2,1)S(1)}, u32[]{:S(2)}, u32[]{:S(2)}) collective-permute-start(bf16[368,1152]{1,0:T(8,128)(2,1)S(1)} %convolution_convert_fusion.3), channel_id=1, source_target_pairs={{0,1},{1,0},{2,3},{3,2},{4,5},{5,4},{6,7},{7,6},{8,9},{9,8},{10,11... | collective-permute-start | bytes 2543624 | tf_op jit(solution)/shard_map/ppermute | solution.py:113
  533.1 26.3 %collective-permute-start.13 = (bf16[368,1152]{1,0:T(8,128)(2,1)S(1)}, bf16[368,1152]{1,0:T(8,128)(2,1)S(1)}, u32[]{:S(2)}, u32[]{:S(2)}) collective-permute-start(bf16[368,1152]{1,0:T(8,128)(2,1)S(1)} %convolution_convert_fusion.4), channel_id=1, source_target_pairs={{0,1},{1,0},{2,3},{3,2},{4,5},{5,4},{6,7},{7,6},{8,9},{9,8},{10,11... | collective-permute-start | bytes 2543624 | tf_op jit(solution)/shard_map/ppermute | solution.py:113
  559.4 46.3 %copy-start.6 = (f32[368,1152]{1,0:T(8,128)S(1)}, f32[368,1152]{1,0:T(8,128)}, u32[]{:S(2)}) copy-start(f32[368,1152]{1,0:T(8,128)} %copy-done.5) | copy-start | bytes 5087236
  (46 other events, 156.5 us)
Sparse Core Ops, SparseCore 0:
  10.9 52.9 all-gather.4
  66.1 37.8 all-gather.6
  106.1 53.7 all-gather.8
  161.8 53.4 all-gather.10
  439.3 57.4 reduce-scatter.12
  500.6 70.9 reduce-scatter.10
  575.6 77.1 reduce-scatter.16
  657.4 76.7 reduce-scatter.14
where the time goes:
time: 747 us; the launch traced here: 743 us
  waiting for transfers between devices  264 us (35%)
  matrix products  253 us (34%)
  other arithmetic  96.3 us (13%)
  local copies, waits for them, and re-layouts  58.3 us (8%)
  blocking collectives  39.7 us (5%)
  starting transfers between devices  16.3 us (2%)
  between operations  15.7 us (2%)
    dot_general x28, matrix products, dot(): lax.dot_general(left, right, (dims, ((), ())), preferred_element_type=jnp...  163 us
    unnamed x11, waiting for transfers between devices  120 us
    ppermute x16, waiting for transfers between devices, swap_halves(): return lax.ppermute(block, 'tp', [(0, 1), (1, 0)])  119 us
    psum x1, blocking collectives, per_device(): total = lax.psum(jnp.concatenate(pieces), ('fsdp', 'tp'))  39.7 us
    convert_element_type x4, local copies, waits for them, and re-layouts, by_shard(): whole.astype(jnp.bfloat16)  26.2 us
    convert_element_type x2, other arithmetic, attend_backward(): d_scores = (probs_full * (d_probs - row_inner)).astype(jnp.bfloat16)  25.8 us
    all_gather x4, waiting for transfers between devices, gather_weight(): return lax.all_gather(shard, 'fsdp', axis=0, tiled=True)  24.9 us
    dot_general x2, matrix products, attend_backward(): jnp.einsum('qhe,khe->hqk', grad_heads, value_heads, preferred_element_typ...  23.6 us
  transfers between devices with their start and end apart: 24, of which 11 were waited for; matrix products, arithmetic and copies ran while one was open for 48% of the time, Pallas kernels for 0%

commit v1 on v0

--- a/solution.py
+++ b/solution.py
@@ -8,6 +8,32 @@
 VALID = 729
 norm_eps = 1e-06
 gelu_coef = math.sqrt(2.0 / math.pi)
+
+
+def table_spread(q_in, in_dim):
+    q_in = jnp.moveaxis(q_in, 0, in_dim)
+    finding = q_in.shape
+    u1 = q_in.reshape(
+        *finding[:in_dim], finding[in_dim] * finding[in_dim + 1], *finding[in_dim + 2 :]
+    )
+    return u1
+
+
+def solve_object(a_name, array_dim, chunk):
+    nodes = lax.psum(1, a_name)
+    sides = [(j0, (j0 + 1) % nodes) for j0 in range(nodes)]
+    trail = [(m, at) for at, m in sides]
+    e_now, mid_arr = ([], [])
+    for num in range(nodes - 1):
+        if num % 2 == 0:
+            e_now.append(lax.ppermute(e_now[-1] if e_now else chunk, a_name, sides))
+        else:
+            mid_arr.append(lax.ppermute(mid_arr[-1] if mid_arr else chunk, a_name, trail))
+    r1 = jnp.stack([*e_now[::-1], chunk, *mid_arr])
+    answer = lax.axis_index(a_name) - len(e_now)
+    r1 = r1[(jnp.arange(nodes) - answer) % nodes]
+    last = table_spread(r1, array_dim)
+    return last
 
 
 def norm_forward(values, scale_row, shift_row):
@@ -130,7 +156,7 @@
 
 
 def gather_weight(shard):
-    return lax.all_gather(shard, "fsdp", axis=0, tiled=True)
+    return solve_object("fsdp", array_dim=0, chunk=shard)
 
 
 def scatter_weight(whole):

time: 747 us -> 906 us (1.21)
  starting transfers between devices: 16.3 us -> 122 us
  local copies, waits for them, and re-layouts: 58.3 us -> 144 us
  waiting for transfers between devices: 264 us -> 232 us
    ppermute x0 -> x60, starting transfers between devices: none -> 99.6 us  [the longest x28 76.2 us: solve_object(): lax.ppermute(mid_arr[-1] if mid_arr else chunk, a_name, trail)]
    unnamed x176 -> x290, local copies, waits for them, and re-layouts: 7.06 us -> 65.2 us
    ppermute x16, waiting for transfers between devices: 119 us -> 63.3 us  [swap_halves(): return lax.ppermute(block, 'tp', [(0, 1), (1, 0)])]
    ppermute x0 -> x60, waiting for transfers between devices: none -> 54.1 us  [the longest x32 47.3 us: solve_object(): e_now.append(lax.ppermute(e_now[-1] if e_now else chunk, a_name, sides))]
    all_gather x4 -> x0, waiting for transfers between devices: 24.9 us -> none  [gather_weight(): return lax.all_gather(shard, 'fsdp', axis=0, tiled=True)]
    gather x0 -> x4, local copies, waits for them, and re-layouts: none -> 18.5 us  [solve_object(): r1 = r1[(jnp.arange(nodes) - answer) % nodes]]
    unnamed x11 -> x7, waiting for transfers between devices: 120 us -> 114 us
  transfers between devices with their start and end apart: 24 -> 80, of which waited for: 11 -> 25; matrix products, arithmetic and copies ran while one was open for 48% -> 49% of each run, Pallas kernels for 0% -> 0%
where the time goes in v1:
time: 906 us; the launch traced here: 896 us
  matrix products  248 us (27%)
  waiting for transfers between devices  232 us (26%)
  local copies, waits for them, and re-layouts  144 us (16%)
  starting transfers between devices  122 us (13%)
  other arithmetic  97.6 us (11%)
  blocking collectives  37.4 us (4%)
  between operations  16 us (2%)
    dot_general x28, matrix products, dot(): lax.dot_general(left, right, (dims, ((), ())), preferred_element_type=jnp...  158 us
    unnamed x7, waiting for transfers between devices  114 us
    ppermute x28, starting transfers between devices, solve_object(): lax.ppermute(mid_arr[-1] if mid_arr else chunk, a_name, trail)  76.2 us
    unnamed x290, local copies, waits for them, and re-layouts  65.2 us
    ppermute x16, waiting for transfers between devices, swap_halves(): return lax.ppermute(block, 'tp', [(0, 1), (1, 0)])  63.3 us
    ppermute x32, waiting for transfers between devices, solve_object(): e_now.append(lax.ppermute(e_now[-1] if e_now else chunk, a_name, sides))  47.3 us
    psum x1, blocking collectives, per_device(): total = lax.psum(jnp.concatenate(pieces), ('fsdp', 'tp'))  37.4 us
    convert_element_type x4, local copies, waits for them, and re-layouts, by_shard(): whole.astype(jnp.bfloat16)  25.9 us
  transfers between devices with their start and end apart: 80, of which 25 were waited for; matrix products, arithmetic and copies ran while one was open for 49% of the time, Pallas kernels for 0%

profile of v1, /device:TPU:0, one launch (start us, length us, event | category | flops | bytes accessed | tf_op | source)
XLA Modules:
  0.0 896.2 jit_solution(12138512964483418607)
XLA Ops:
  7.3 5.5 collective-permute-start.24
  16.5 4.4 collective-permute-start.9
  21.0 4.4 collective-permute-start.56
  30.1 6.6 collective-permute-done.17
  36.8 6.6 collective-permute-done.18
  45.3 4.9 collective-permute-done.19
  51.6 4.5 collective-permute-start.25
  60.9 4.4 collective-permute-start.26
  67.5 4.6 collective-permute-start.27
  74.2 4.6 collective-permute-start.28
  83.1 5.0 collective-permute-done.3
  90.0 6.6 collective-permute-done.4
  97.6 7.5 collective-permute-done.5
  106.2 4.4 collective-permute-start.41
  116.3 4.6 collective-permute-start.30
  123.4 4.3 collective-permute-start.13
  129.7 4.5 collective-permute-start.42
  171.6 4.4 collective-permute-start.15
  184.1 4.8 collective-permute-start.52
  192.3 5.0 gather_fusion
  200.9 5.2 collective-permute-start.38
  206.1 6.0 add_convert_fusion
  224.3 6.3 add_convert_fusion.1
  239.1 9.4 %fusion.187 = (f32[8,736]{1,0:T(8,128)S(1)}, f32[8,736,736]{1,2,0:T(8,128)}) fusion(bf16[736,8,72]{0,2,1:T(8,128)(2,1)} %bitcast.351, bf16[736,8,72]{0,2,1:T(8,128)(2,1)S(1)} %bitcast.341, pred[736]{0:T(1024)(128)(4,1)S(1)} %copy-done.107), kind=kOutput, calls=%fused_computation.364 | convolution fusion | flops 637028608 | bytes 19054304 | tf_op jit(solution)/shard_map/qhe,khe->hqk/dot_general | solution.py:76
  248.4 8.8 fusion
  257.2 9.1 %fusion.147 = bf16[8,72,736]{2,1,0:T(8,128)(2,1)} fusion(bf16[736,8,72]{0,2,1:T(8,128)(2,1)S(1)} %bitcast.382, f32[8,736,736]{1,2,0:T(8,128)} %get-tuple-element.106, f32[8,736]{1,0:T(8,128)S(1)} %fusion, f32[8,736]{1,0:T(8,128)S(1)} %get-tuple-element.105), kind=kOutput, calls=%fused_computation.219 | convolution fusion | flops 637458432 | bytes 19077120 | tf_op jit(solution)/shard_map/hqk,khe->qhe/dot_general | solution.py:90
  266.3 8.3 fusion.186
  274.6 8.8 fusion.1
  283.4 8.7 fusion.146
  315.6 4.7 collective-permute-start.31
  342.2 17.7 %collective-permute-done.65 = bf16[368,1152]{1,0:T(8,128)(2,1)S(1)} collective-permute-done((bf16[368,1152]{1,0:T(8,128)(2,1)S(1)}, bf16[368,1152]{1,0:T(8,128)(2,1)S(1)}, u32[]{:S(2)}, u32[]{:S(2)}) %collective-permute-start.65) | collective-permute-done | bytes 847904 | tf_op jit(solution)/shard_map/ppermute | solution.py:139
  365.9 5.9 gather_fusion.2
  373.6 5.8 gather_fusion.3
  379.4 5.6 collective-permute-done.66
  384.9 10.0 %fusion.120 = f32[736,2152]{1,0:T(8,128)} fusion(bf16[1152,2152]{1,0:T(8,128)(2,1)} %bitcast.366, bf16[368,1152]{1,0:T(8,128)(2,1)} %collective-permute-done.66, bf16[368,1152]{1,0:T(8,128)(2,1)S(1)} %get-tuple-element.96), kind=kOutput, calls=%fused_computation.175 | convolution fusion | flops 3652632576 | bytes 12989440 | tf_op jit(solution)/shard_map/dot_general | solution.py:130
  395.0 9.7 %fusion.27 = bf16[736,2152]{1,0:T(8,128)(2,1)S(1)} fusion(bf16[1152,2152]{1,0:T(8,128)(2,1)S(1)} %bitcast.364, f32[736,2152]{1,0:T(8,128)} %fusion.120, f32[2152]{0:T(1024)S(1)} %dynamic_slice.17, bf16[368,1152]{1,0:T(8,128)(2,1)} %collective-permute-done.69, bf16[368,1152]{1,0:T(8,128)(2,1)} %get-tuple-element.80), kind=kOutput, calls=%fused_computation.50 | convolution fusion | flops 3684310016 | bytes 16165792 | tf_op jit(solution)/shard_map/dot_general | solution.py:130
  410.1 11.3 %multiply_convert_fusion.3 = (bf16[736,2152]{1,0:T(8,128)(2,1)S(1)}, bf16[736,2152]{1,0:T(8,128)(2,1)}, f32[736,2152]{1,0:T(8,128)}) fusion(f32[2152]{0:T(1024)S(1)} %dynamic_slice.17, f32[736,2152]{1,0:T(8,128)} %fusion.120, bf16[1152,2152]{1,0:T(8,128)(2,1)S(1)} %bitcast.372, bf16[368,1152]{1,0:T(8,128)(2,1)S(1)} %collective-permute-done.32, ...), kind=kOutput, calls=%fused_computation.56 | convolution fusion | flops 3684310016 | bytes 25669024 | tf_op jit(solution)/shard_map/dot_general | solution.py:130
  421.4 10.6 %fusion.21 = bf16[736,2152]{1,0:T(8,128)(2,1)S(1)} fusion(bf16[1152,2152]{1,0:T(8,128)(2,1)S(1)} %bitcast.365, f32[736,2152]{1,0:T(8,128)} %get-tuple-element.111, f32[2152]{0:T(1024)S(1)} %dynamic_slice.17, bf16[368,1152]{1,0:T(8,128)(2,1)} %collective-permute-done.68, bf16[368,1152]{1,0:T(8,128)(2,1)S(1)} %copy-done.49), kind=kOutput, calls=%fused_computation.44 | convolution fusion | flops 3684310016 | bytes 16165792 | tf_op jit(solution)/shard_map/dot_general | solution.py:130
  435.4 13.5 %convolution_convert_fusion = bf16[1152,2152]{0,1:T(8,128)(2,1)} fusion(bf16[736,2152]{1,0:T(8,128)(2,1)S(1)} %fusion.27, bf16[736,2152]{1,0:T(8,128)(2,1)S(1)} %fusion.21, bf16[368,1152]{1,0:T(8,128)(2,1)} %collective-permute-done.66, bf16[368,1152]{1,0:T(8,128)(2,1)S(1)} %get-tuple-element.96, bf16[368,1152]{1,0:T(8,128)(2,1)S(1)} %collective-permute-done.32, ...), kind=kOutput, calls=%fused_computation.21 | convolution fusion | flops 7327198208 | bytes 14685184 | tf_op jit(solution)/shard_map/dot_general | solution.py:130
  448.9 14.1 %convolution_convert_fusion.1 = bf16[1152,2152]{0,1:T(8,128)(2,1)} fusion(bf16[736,2152]{1,0:T(8,128)(2,1)} %get-tuple-element.98, bf16[736,2152]{1,0:T(8,128)(2,1)S(1)} %get-tuple-element.97, bf16[368,1152]{1,0:T(8,128)(2,1)} %collective-permute-done.69, bf16[368,1152]{1,0:T(8,128)(2,1)} %get-tuple-element.80, ...), kind=kOutput, calls=%fused_computation.22 | convolution fusion | flops 7327198208 | bytes 14685184 | tf_op jit(solution)/shard_map/dot_general | solution.py:130
  463.0 8.4 copy.73
  471.4 8.4 copy.72
  479.9 6.8 convolution_add_fusion.4
  486.7 6.4 convolution_add_fusion.5
  501.9 19.6 %collective-permute-done.74 = bf16[368,1152]{1,0:T(8,128)(2,1)S(1)} collective-permute-done((bf16[368,1152]{1,0:T(8,128)(2,1)S(1)}, bf16[368,1152]{1,0:T(8,128)(2,1)S(1)}, u32[]{:S(2)}, u32[]{:S(2)}) %collective-permute-start.74) | collective-permute-done | bytes 847904 | tf_op jit(solution)/shard_map/ppermute | solution.py:139
  522.9 11.6 %multiply_reduce_fusion = (f32[8,736]{1,0:T(8,128)S(1)}, f32[8,736,736]{1,2,0:T(8,128)}) fusion(f32[8,736,736]{1,2,0:T(8,128)} %get-tuple-element.104, f32[8,736]{1,0:T(8,128)S(1)} %log_add_fusion, bf16[736,8,72]{0,2,1:T(8,128)(2,1)S(1)} %bitcast.384, bf16[736,8,72]{0,2,1:T(8,128)(2,1)S(1)} %bitcast.381), kind=kOutput, calls=%fused_computation.5 | convolution fusion | flops 637028608 | bytes 36411392 | tf_op jit(solution)/shard_map/qhe,khe->hqk/dot_general | solution.py:103
  534.5 12.6 %multiply_convert_fusion = bf16[8,736,736]{1,2,0:T(8,128)(2,1)S(1)} fusion(f32[8,736,736]{1,2,0:T(8,128)} %get-tuple-element.115, f32[8,736,736]{1,2,0:T(8,128)} %get-tuple-element.104, f32[8,736]{1,0:T(8,128)S(1)} %get-tuple-element.114, f32[8,736]{1,0:T(8,128)S(1)} %log_add_fusion), kind=kLoop, calls=%fused_computation.4 | loop fusion | flops 17334272 | bytes 43382784 | tf_op jit(solution)/shard_map/convert_element_type | solution.py:107
  553.4 9.9 %fusion.151 = bf16[8,72,736]{2,1,0:T(8,128)(2,1)} fusion(bf16[736,8,72]{0,2,1:T(8,128)(2,1)S(1)} %bitcast.385, f32[8,736,736]{1,2,0:T(8,128)} %get-tuple-element.104, f32[8,736]{1,0:T(8,128)S(1)} %log_add_fusion), kind=kOutput, calls=%fused_computation.221 | convolution fusion | flops 633124864 | bytes 19053568 | tf_op jit(solution)/shard_map/hqk,qhe->khe/dot_general | solution.py:108
  564.8 9.9 %fusion.148 = bf16[8,72,736]{2,1,0:T(8,128)(2,1)} fusion(bf16[736,8,72]{0,2,1:T(8,128)(2,1)S(1)} %bitcast.386, f32[8,736,736]{1,2,0:T(8,128)} %get-tuple-element.106, f32[8,736]{1,0:T(8,128)S(1)} %log_add_fusion.1), kind=kOutput, calls=%fused_computation.220 | convolution fusion | flops 633124864 | bytes 19053568 | tf_op jit(solution)/shard_map/hqk,qhe->khe/dot_general | solution.py:108
  574.7 12.0 %multiply_reduce_fusion.1 = (f32[8,736]{1,0:T(8,128)S(1)}, f32[8,736,736]{1,2,0:T(8,128)}) fusion(f32[8,736,736]{1,2,0:T(8,128)} %get-tuple-element.106, f32[8,736]{1,0:T(8,128)S(1)} %log_add_fusion.1, bf16[736,8,72]{0,2,1:T(8,128)(2,1)S(1)} %bitcast.387, bf16[736,8,72]{0,2,1:T(8,128)(2,1)S(1)} %bitcast.383), kind=kOutput, calls=%fused_computation.8 | convolution fusion | flops 637028608 | bytes 36411392 | tf_op jit(solution)/shard_map/qhe,khe->hqk/dot_general | solution.py:103
  593.0 13.2 %multiply_convert_fusion.1 = bf16[8,736,736]{1,2,0:T(8,128)(2,1)S(1)} fusion(f32[8,736,736]{1,2,0:T(8,128)} %get-tuple-element.113, f32[8,736,736]{1,2,0:T(8,128)} %get-tuple-element.106, f32[8,736]{1,0:T(8,128)S(1)} %get-tuple-element.112, f32[8,736]{1,0:T(8,128)S(1)} %log_add_fusion.1), kind=kLoop, calls=%fused_computation.7 | loop fusion | flops 17334272 | bytes 43382784 | tf_op jit(solution)/shard_map/convert_element_type | solution.py:107
  611.7 10.9 %convolution_convert_fusion.2 = bf16[1152,1728]{0,1:T(8,128)(2,1)} fusion(bf16[368,1152]{1,0:T(8,128)(2,1)} %collective-permute-done.64, bf16[368,1152]{1,0:T(8,128)(2,1)S(1)} %copy-done.51, bf16[368,1152]{1,0:T(8,128)(2,1)} %collective-permute-done, bf16[368,1152]{1,0:T(8,128)(2,1)} %get-tuple-element.73, bf16[736,576]{0,1:T(8,128)(2,1)S(1)} %bitcast.354, ...), kind=kOutput, calls=%fused_computation.34 | convolution fusion | flops 5906571264 | bytes 12460032 | tf_op jit(solution)/shard_map/dot_general | solution.py:130
  622.6 6.4 copy.80
  631.8 6.3 convolution_convert_fusion.7
  640.0 5.7 convolution_convert_fusion.9
  647.4 12.8 %collective-permute-done.67 = bf16[368,1152]{1,0:T(8,128)(2,1)} collective-permute-done((bf16[368,1152]{1,0:T(8,128)(2,1)}, bf16[368,1152]{1,0:T(8,128)(2,1)}, u32[]{:S(2)}, u32[]{:S(2)}) %collective-permute-start.67) | collective-permute-done | bytes 847904 | tf_op jit(solution)/shard_map/ppermute | solution.py:139
  660.2 6.1 fusion.73
  666.3 5.6 collective-permute-done.63
  672.0 5.1 fusion.74
  689.7 23.3 %convert_reduce_fusion.1 = f32[1728]{0:T(1024)S(1)} fusion(bf16[736,576]{0,1:T(8,128)(2,1)S(1)} %bitcast.355, bf16[736,576]{0,1:T(8,128)(2,1)S(1)} %bitcast.345, bf16[736,576]{0,1:T(8,128)(2,1)S(1)} %bitcast.335, bf16[736,576]{0,1:T(8,128)(2,1)S(1)} %bitcast.358, bf16[736,576]{0,1:T(8,128)(2,1)S(1)} %bitcast.348, bf16[736,576]{0,1:T(8,128)(2,1)S(1)} %bitcast.338), kind=kLoop, calls=%fused_computation.23 | loop fusion | flops 33065280 | bytes 5094144 | tf_op jit(solution)/shard_map/reduce_sum | solution.py:250
  717.5 4.9 fusion.108
  722.7 37.4 %psum.7 = f32[13520]{0:T(1024)S(1)} all-reduce(f32[13520]{0:T(1024)S(1)} %constant_dynamic-update-slice_fusion.18), channel_id=1, replica_groups=mesh['fsdp'=16,'tp'=2] {'fsdp','tp'}, use_global_device_ids=true, to_apply=%region_39.40 | all-reduce | flops 13520 | bytes 108160 | tf_op jit(solution)/shard_map/psum | solution.py:278
  772.2 33.8 %reduce-scatter.17.cloned.1.call-done = bf16[1,72,2152]{2,1,0:T(8,128)(2,1)} async-done(((bf16[16,72,2152]{2,1,0:T(8,128)(2,1)}), bf16[1,72,2152]{2,1,0:T(8,128)(2,1)}) %reduce-scatter.17.cloned.1.call-update) | async-done | bytes 309904
  807.9 79.5 %reduce-scatter.15.cloned.1.call-done = bf16[1,72,2152]{2,1,0:T(8,128)(2,1)} async-done(((bf16[16,72,2152]{2,1,0:T(8,128)(2,1)}), bf16[1,72,2152]{2,1,0:T(8,128)(2,1)}) %reduce-scatter.15.cloned.1.call-update) | async-done | bytes 309904
  (535 shorter events, 242.2 us)
Async XLA Ops:
  7.2 761.3 %reduce-scatter.13.cloned.1.call-start = ((), (), s32[]{:S(2)}) async-start(), calls=%async_computation.5 | async-start | bytes 1566720
  7.3 44.3 %collective-permute-start.24 = (bf16[72,576]{1,0:T(8,128)(2,1)}, bf16[72,576]{1,0:T(8,128)(2,1)}, u32[]{:S(2)}, u32[]{:S(2)}) collective-permute-start(bf16[72,576]{1,0:T(8,128)(2,1)} %bitcast.406), channel_id=1, source_target_pairs={{2,0},{4,2},{6,4},{8,6},{10,8},{12,10},{14,12},{16,14},{18,16},{20... | collective-permute-start | bytes 248840 | tf_op jit(solution)/shard_map/ppermute | solution.py:31
  12.7 17.2 %collective-permute-start.16 = (bf16[72,576]{1,0:T(8,128)(2,1)}, bf16[72,576]{1,0:T(8,128)(2,1)S(1)}, u32[]{:S(2)}, u32[]{:S(2)}) collective-permute-start(bf16[72,576]{1,0:T(8,128)(2,1)} %bitcast.407), channel_id=1, source_target_pairs={{0,2},{2,4},{4,6},{6,8},{8,10},{10,12},{12,14},{14,16},{16,18},{18... | collective-permute-start | bytes 248840 | tf_op jit(solution)/shard_map/ppermute | solution.py:29
  16.5 39.6 %collective-permute-start.9 = (bf16[72,1728]{1,0:T(8,128)(2,1)}, bf16[72,1728]{1,0:T(8,128)(2,1)}, u32[]{:S(2)}, u32[]{:S(2)}) collective-permute-start(bf16[72,1728]{1,0:T(8,128)(2,1)} %reshape.279), channel_id=1, source_target_pairs={{2,0},{4,2},{6,4},{8,6},{10,8},{12,10},{14,12},{16,14},{18,16},{20... | collective-permute-start | bytes 746504 | tf_op jit(solution)/shard_map/ppermute | solution.py:31
  21.0 35.2 %collective-permute-start.1 = (bf16[72,1728]{1,0:T(8,128)(2,1)}, bf16[72,1728]{1,0:T(8,128)(2,1)}, u32[]{:S(2)}, u32[]{:S(2)}) collective-permute-start(bf16[72,1728]{1,0:T(8,128)(2,1)} %reshape.279), channel_id=1, source_target_pairs={{0,2},{2,4},{4,6},{6,8},{8,10},{10,12},{12,14},{14,16},{16,18},{18... | collective-permute-start | bytes 746504 | tf_op jit(solution)/shard_map/ppermute | solution.py:29
  21.0 85.2 %collective-permute-start.56 = (bf16[72,2152]{1,0:T(8,128)(2,1)}, bf16[72,2152]{1,0:T(8,128)(2,1)}, u32[]{:S(2)}, u32[]{:S(2)}) collective-permute-start(bf16[72,2152]{1,0:T(8,128)(2,1)} %bitcast.403), channel_id=1, source_target_pairs={{2,0},{4,2},{6,4},{8,6},{10,8},{12,10},{14,12},{16,14},{18,16},{20... | collective-permute-start | bytes 929672 | tf_op jit(solution)/shard_map/ppermute | solution.py:31
  51.6 9.3 %collective-permute-start.25 = (bf16[72,576]{1,0:T(8,128)(2,1)}, bf16[72,576]{1,0:T(8,128)(2,1)S(1)}, u32[]{:S(2)}, u32[]{:S(2)}) collective-permute-start(bf16[72,576]{1,0:T(8,128)(2,1)} %collective-permute-done.24), channel_id=1, source_target_pairs={{2,0},{4,2},{6,4},{8,6},{10,8},{12,10},{14,12},{16,14},{18,16},{20... | collective-permute-start | bytes 248840 | tf_op jit(solution)/shard_map/ppermute | solution.py:31
  56.1 18.2 %collective-permute-start.10 = (bf16[72,1728]{1,0:T(8,128)(2,1)}, bf16[72,1728]{1,0:T(8,128)(2,1)}, u32[]{:S(2)}, u32[]{:S(2)}) collective-permute-start(bf16[72,1728]{1,0:T(8,128)(2,1)} %collective-permute-done.9), channel_id=1, source_target_pairs={{2,0},{4,2},{6,4},{8,6},{10,8},{12,10},{14,12},{16,14},{18,16},{20... | collective-permute-start | bytes 746504 | tf_op jit(solution)/shard_map/ppermute | solution.py:31
  56.2 22.7 %collective-permute-start.2 = (bf16[72,1728]{1,0:T(8,128)(2,1)}, bf16[72,1728]{1,0:T(8,128)(2,1)}, u32[]{:S(2)}, u32[]{:S(2)}) collective-permute-start(bf16[72,1728]{1,0:T(8,128)(2,1)} %collective-permute-done.1), channel_id=1, source_target_pairs={{0,2},{2,4},{4,6},{6,8},{8,10},{10,12},{12,14},{14,16},{16,18},{18... | collective-permute-start | bytes 746504 | tf_op jit(solution)/shard_map/ppermute | solution.py:29
  74.2 32.0 %collective-permute-start.48 = (bf16[72,2152]{1,0:T(8,128)(2,1)}, bf16[72,2152]{1,0:T(8,128)(2,1)}, u32[]{:S(2)}, u32[]{:S(2)}) collective-permute-start(bf16[72,2152]{1,0:T(8,128)(2,1)} %bitcast.404), channel_id=1, source_target_pairs={{0,2},{2,4},{4,6},{6,8},{8,10},{10,12},{12,14},{14,16},{16,18},{18... | collective-permute-start | bytes 929672 | tf_op jit(solution)/shard_map/ppermute | solution.py:29
  74.2 36.4 %collective-permute-start.28 = (bf16[72,576]{1,0:T(8,128)(2,1)S(1)}, bf16[72,576]{1,0:T(8,128)(2,1)S(1)}, u32[]{:S(2)}, u32[]{:S(2)}) collective-permute-start(bf16[72,576]{1,0:T(8,128)(2,1)S(1)} %collective-permute-done.27), channel_id=1, source_target_pairs={{2,0},{4,2},{6,4},{8,6},{10,8},{12,10},{14,12},{16,14},{18,16},{20... | collective-permute-start | bytes 248840 | tf_op jit(solution)/shard_map/ppermute | solution.py:31
  78.9 32.2 %collective-permute-start.11 = (bf16[72,1728]{1,0:T(8,128)(2,1)}, bf16[72,1728]{1,0:T(8,128)(2,1)S(1)}, u32[]{:S(2)}, u32[]{:S(2)}) collective-permute-start(bf16[72,1728]{1,0:T(8,128)(2,1)} %collective-permute-done.10), channel_id=1, source_target_pairs={{2,0},{4,2},{6,4},{8,6},{10,8},{12,10},{14,12},{16,14},{18,16},{20... | collective-permute-start | bytes 746504 | tf_op jit(solution)/shard_map/ppermute | solution.py:31
  106.1 14.8 %collective-permute-start.33 = (bf16[72,2152]{1,0:T(8,128)(2,1)}, bf16[72,2152]{1,0:T(8,128)(2,1)}, u32[]{:S(2)}, u32[]{:S(2)}) collective-permute-start(bf16[72,2152]{1,0:T(8,128)(2,1)} %param.12), channel_id=1, source_target_pairs={{0,2},{2,4},{4,6},{6,8},{8,10},{10,12},{12,14},{14,16},{16,18},{18... | collective-permute-start | bytes 929672 | tf_op jit(solution)/shard_map/ppermute | solution.py:29
  106.2 14.8 %collective-permute-start.41 = (bf16[72,2152]{1,0:T(8,128)(2,1)}, bf16[72,2152]{1,0:T(8,128)(2,1)S(1)}, u32[]{:S(2)}, u32[]{:S(2)}) collective-permute-start(bf16[72,2152]{1,0:T(8,128)(2,1)} %param.12), channel_id=1, source_target_pairs={{2,0},{4,2},{6,4},{8,6},{10,8},{12,10},{14,12},{16,14},{18,16},{20... | collective-permute-start | bytes 929672 | tf_op jit(solution)/shard_map/ppermute | solution.py:31
  111.1 12.3 %collective-permute-start.12 = (bf16[72,1728]{1,0:T(8,128)(2,1)S(1)}, bf16[72,1728]{1,0:T(8,128)(2,1)}, u32[]{:S(2)}, u32[]{:S(2)}) collective-permute-start(bf16[72,1728]{1,0:T(8,128)(2,1)S(1)} %collective-permute-done.11), channel_id=1, source_target_pairs={{2,0},{4,2},{6,4},{8,6},{10,8},{12,10},{14,12},{16,14},{18,16},{20... | collective-permute-start | bytes 746504 | tf_op jit(solution)/shard_map/ppermute | solution.py:31
  113.7 14.0 %collective-permute-start.7 = (bf16[72,1728]{1,0:T(8,128)(2,1)S(1)}, bf16[72,1728]{1,0:T(8,128)(2,1)}, u32[]{:S(2)}, u32[]{:S(2)}) collective-permute-start(bf16[72,1728]{1,0:T(8,128)(2,1)S(1)} %collective-permute-done.6), channel_id=1, source_target_pairs={{0,2},{2,4},{4,6},{6,8},{8,10},{10,12},{12,14},{14,16},{16,18},{18... | collective-permute-start | bytes 746504 | tf_op jit(solution)/shard_map/ppermute | solution.py:29
  121.0 13.2 %collective-permute-start.49 = (bf16[72,2152]{1,0:T(8,128)(2,1)}, bf16[72,2152]{1,0:T(8,128)(2,1)}, u32[]{:S(2)}, u32[]{:S(2)}) collective-permute-start(bf16[72,2152]{1,0:T(8,128)(2,1)} %collective-permute-done.48), channel_id=1, source_target_pairs={{0,2},{2,4},{4,6},{6,8},{8,10},{10,12},{12,14},{14,16},{16,18},{18... | collective-permute-start | bytes 929672 | tf_op jit(solution)/shard_map/ppermute | solution.py:29
  123.0 14.0 %collective-permute-start.34 = (bf16[72,2152]{1,0:T(8,128)(2,1)}, bf16[72,2152]{1,0:T(8,128)(2,1)}, u32[]{:S(2)}, u32[]{:S(2)}) collective-permute-start(bf16[72,2152]{1,0:T(8,128)(2,1)} %collective-permute-done.33), channel_id=1, source_target_pairs={{0,2},{2,4},{4,6},{6,8},{8,10},{10,12},{12,14},{14,16},{16,18},{18... | collective-permute-start | bytes 929672 | tf_op jit(solution)/shard_map/ppermute | solution.py:29
  123.4 17.1 %collective-permute-start.13 = (bf16[72,1728]{1,0:T(8,128)(2,1)}, bf16[72,1728]{1,0:T(8,128)(2,1)}, u32[]{:S(2)}, u32[]{:S(2)}) collective-permute-start(bf16[72,1728]{1,0:T(8,128)(2,1)} %collective-permute-done.12), channel_id=1, source_target_pairs={{2,0},{4,2},{6,4},{8,6},{10,8},{12,10},{14,12},{16,14},{18,16},{20... | collective-permute-start | bytes 746504 | tf_op jit(solution)/shard_map/ppermute | solution.py:31
  127.7 15.3 %collective-permute-start.8 = (bf16[72,1728]{1,0:T(8,128)(2,1)}, bf16[72,1728]{1,0:T(8,128)(2,1)}, u32[]{:S(2)}, u32[]{:S(2)}) collective-permute-start(bf16[72,1728]{1,0:T(8,128)(2,1)} %collective-permute-done.7), channel_id=1, source_target_pairs={{0,2},{2,4},{4,6},{6,8},{8,10},{10,12},{12,14},{14,16},{16,18},{18... | collective-permute-start | bytes 746504 | tf_op jit(solution)/shard_map/ppermute | solution.py:29
  129.7 36.8 %collective-permute-start.42 = (bf16[72,2152]{1,0:T(8,128)(2,1)}, bf16[72,2152]{1,0:T(8,128)(2,1)S(1)}, u32[]{:S(2)}, u32[]{:S(2)}) collective-permute-start(bf16[72,2152]{1,0:T(8,128)(2,1)} %copy-done.54), channel_id=1, source_target_pairs={{2,0},{4,2},{6,4},{8,6},{10,8},{12,10},{14,12},{16,14},{18,16},{20... | collective-permute-start | bytes 929672 | tf_op jit(solution)/shard_map/ppermute | solution.py:31
  134.2 33.8 %collective-permute-start.58 = (bf16[72,2152]{1,0:T(8,128)(2,1)}, bf16[72,2152]{1,0:T(8,128)(2,1)S(1)}, u32[]{:S(2)}, u32[]{:S(2)}) collective-permute-start(bf16[72,2152]{1,0:T(8,128)(2,1)} %collective-permute-done.57), channel_id=1, source_target_pairs={{2,0},{4,2},{6,4},{8,6},{10,8},{12,10},{14,12},{16,14},{18,16},{20... | collective-permute-start | bytes 929672 | tf_op jit(solution)/shard_map/ppermute | solution.py:31
  137.0 34.5 %collective-permute-start.50 = (bf16[72,2152]{1,0:T(8,128)(2,1)}, bf16[72,2152]{1,0:T(8,128)(2,1)S(1)}, u32[]{:S(2)}, u32[]{:S(2)}) collective-permute-start(bf16[72,2152]{1,0:T(8,128)(2,1)} %collective-permute-done.49), channel_id=1, source_target_pairs={{0,2},{2,4},{4,6},{6,8},{8,10},{10,12},{12,14},{14,16},{16,18},{18... | collective-permute-start | bytes 929672 | tf_op jit(solution)/shard_map/ppermute | solution.py:29
  140.5 31.0 %collective-permute-start.35 = (bf16[72,2152]{1,0:T(8,128)(2,1)}, bf16[72,2152]{1,0:T(8,128)(2,1)S(1)}, u32[]{:S(2)}, u32[]{:S(2)}) collective-permute-start(bf16[72,2152]{1,0:T(8,128)(2,1)} %collective-permute-done.34), channel_id=1, source_target_pairs={{0,2},{2,4},{4,6},{6,8},{8,10},{10,12},{12,14},{14,16},{16,18},{18... | collective-permute-start | bytes 929672 | tf_op jit(solution)/shard_map/ppermute | solution.py:29
  143.0 28.6 %collective-permute-start.14 = (bf16[72,1728]{1,0:T(8,128)(2,1)}, bf16[72,1728]{1,0:T(8,128)(2,1)S(1)}, u32[]{:S(2)}, u32[]{:S(2)}) collective-permute-start(bf16[72,1728]{1,0:T(8,128)(2,1)} %collective-permute-done.13), channel_id=1, source_target_pairs={{2,0},{4,2},{6,4},{8,6},{10,8},{12,10},{14,12},{16,14},{18,16},{20... | collective-permute-start | bytes 746504 | tf_op jit(solution)/shard_map/ppermute | solution.py:31
  166.4 30.8 %collective-permute-start.64 = (bf16[368,1152]{1,0:T(8,128)(2,1)S(1)}, bf16[368,1152]{1,0:T(8,128)(2,1)}, u32[]{:S(2)}, u32[]{:S(2)}) collective-permute-start(bf16[368,1152]{1,0:T(8,128)(2,1)S(1)} %copy-done.50), channel_id=1, source_target_pairs={{0,1},{1,0},{2,3},{3,2},{4,5},{5,4},{6,7},{7,6},{8,9},{9,8},{10,11... | collective-permute-start | bytes 2543624 | tf_op jit(solution)/shard_map/ppermute | solution.py:139
  168.0 8.8 collective-permute-start.43
  171.5 9.2 %collective-permute-start.51 = (bf16[72,2152]{1,0:T(8,128)(2,1)S(1)}, bf16[72,2152]{1,0:T(8,128)(2,1)S(1)}, u32[]{:S(2)}, u32[]{:S(2)}) collective-permute-start(bf16[72,2152]{1,0:T(8,128)(2,1)S(1)} %collective-permute-done.50), channel_id=1, source_target_pairs={{0,2},{2,4},{4,6},{6,8},{8,10},{10,12},{12,14},{14,16},{16,18},{18... | collective-permute-start | bytes 929672 | tf_op jit(solution)/shard_map/ppermute | solution.py:29
  171.6 12.6 %collective-permute-start.36 = (bf16[72,2152]{1,0:T(8,128)(2,1)S(1)}, bf16[72,2152]{1,0:T(8,128)(2,1)}, u32[]{:S(2)}, u32[]{:S(2)}) collective-permute-start(bf16[72,2152]{1,0:T(8,128)(2,1)S(1)} %collective-permute-done.35), channel_id=1, source_target_pairs={{0,2},{2,4},{4,6},{6,8},{8,10},{10,12},{12,14},{14,16},{16,18},{18... | collective-permute-start | bytes 929672 | tf_op jit(solution)/shard_map/ppermute | solution.py:29
  171.6 17.3 %collective-permute-start.15 = (bf16[72,1728]{1,0:T(8,128)(2,1)S(1)}, bf16[72,1728]{1,0:T(8,128)(2,1)S(1)}, u32[]{:S(2)}, u32[]{:S(2)}) collective-permute-start(bf16[72,1728]{1,0:T(8,128)(2,1)S(1)} %collective-permute-done.14), channel_id=1, source_target_pairs={{2,0},{4,2},{6,4},{8,6},{10,8},{12,10},{14,12},{16,14},{18,16},{20... | collective-permute-start | bytes 746504 | tf_op jit(solution)/shard_map/ppermute | solution.py:31
  176.8 21.0 %collective-permute-start.59 = (bf16[72,2152]{1,0:T(8,128)(2,1)S(1)}, bf16[72,2152]{1,0:T(8,128)(2,1)}, u32[]{:S(2)}, u32[]{:S(2)}) collective-permute-start(bf16[72,2152]{1,0:T(8,128)(2,1)S(1)} %collective-permute-done.58), channel_id=1, source_target_pairs={{2,0},{4,2},{6,4},{8,6},{10,8},{12,10},{14,12},{16,14},{18,16},{20... | collective-permute-start | bytes 929672 | tf_op jit(solution)/shard_map/ppermute | solution.py:31
  180.7 18.7 %collective-permute-start.44 = (bf16[72,2152]{1,0:T(8,128)(2,1)S(1)}, bf16[72,2152]{1,0:T(8,128)(2,1)}, u32[]{:S(2)}, u32[]{:S(2)}) collective-permute-start(bf16[72,2152]{1,0:T(8,128)(2,1)S(1)} %collective-permute-done.43), channel_id=1, source_target_pairs={{2,0},{4,2},{6,4},{8,6},{10,8},{12,10},{14,12},{16,14},{18,16},{20... | collective-permute-start | bytes 929672 | tf_op jit(solution)/shard_map/ppermute | solution.py:31
  184.1 16.7 %collective-permute-start.52 = (bf16[72,2152]{1,0:T(8,128)(2,1)S(1)}, bf16[72,2152]{1,0:T(8,128)(2,1)}, u32[]{:S(2)}, u32[]{:S(2)}) collective-permute-start(bf16[72,2152]{1,0:T(8,128)(2,1)S(1)} %collective-permute-done.51), channel_id=1, source_target_pairs={{0,2},{2,4},{4,6},{6,8},{8,10},{10,12},{12,14},{14,16},{16,18},{18... | collective-permute-start | bytes 929672 | tf_op jit(solution)/shard_map/ppermute | solution.py:29
  188.9 11.9 %collective-permute-start.37 = (bf16[72,2152]{1,0:T(8,128)(2,1)}, bf16[72,2152]{1,0:T(8,128)(2,1)}, u32[]{:S(2)}, u32[]{:S(2)}) collective-permute-start(bf16[72,2152]{1,0:T(8,128)(2,1)} %collective-permute-done.36), channel_id=1, source_target_pairs={{0,2},{2,4},{4,6},{6,8},{8,10},{10,12},{12,14},{14,16},{16,18},{18... | collective-permute-start | bytes 929672 | tf_op jit(solution)/shard_map/ppermute | solution.py:29
  197.2 22.5 %collective-permute-start = (bf16[368,1152]{1,0:T(8,128)(2,1)}, bf16[368,1152]{1,0:T(8,128)(2,1)}, u32[]{:S(2)}, u32[]{:S(2)}) collective-permute-start(bf16[368,1152]{1,0:T(8,128)(2,1)} %get-tuple-element.73), channel_id=1, source_target_pairs={{0,1},{1,0},{2,3},{3,2},{4,5},{5,4},{6,7},{7,6},{8,9},{9,8},{10,11... | collective-permute-start | bytes 2543624 | tf_op jit(solution)/shard_map/ppermute | solution.py:139
  197.8 22.5 %collective-permute-start.60 = (bf16[72,2152]{1,0:T(8,128)(2,1)}, bf16[72,2152]{1,0:T(8,128)(2,1)}, u32[]{:S(2)}, u32[]{:S(2)}) collective-permute-start(bf16[72,2152]{1,0:T(8,128)(2,1)} %collective-permute-done.59), channel_id=1, source_target_pairs={{2,0},{4,2},{6,4},{8,6},{10,8},{12,10},{14,12},{16,14},{18,16},{20... | collective-permute-start | bytes 929672 | tf_op jit(solution)/shard_map/ppermute | solution.py:31
  199.4 21.4 %collective-permute-start.45 = (bf16[72,2152]{1,0:T(8,128)(2,1)}, bf16[72,2152]{1,0:T(8,128)(2,1)}, u32[]{:S(2)}, u32[]{:S(2)}) collective-permute-start(bf16[72,2152]{1,0:T(8,128)(2,1)} %collective-permute-done.44), channel_id=1, source_target_pairs={{2,0},{4,2},{6,4},{8,6},{10,8},{12,10},{14,12},{16,14},{18,16},{20... | collective-permute-start | bytes 929672 | tf_op jit(solution)/shard_map/ppermute | solution.py:31
  200.9 20.7 %collective-permute-start.53 = (bf16[72,2152]{1,0:T(8,128)(2,1)}, bf16[72,2152]{1,0:T(8,128)(2,1)}, u32[]{:S(2)}, u32[]{:S(2)}) collective-permute-start(bf16[72,2152]{1,0:T(8,128)(2,1)} %collective-permute-done.52), channel_id=1, source_target_pairs={{0,2},{2,4},{4,6},{6,8},{8,10},{10,12},{12,14},{14,16},{16,18},{18... | collective-permute-start | bytes 929672 | tf_op jit(solution)/shard_map/ppermute | solution.py:29
  200.9 21.8 %collective-permute-start.38 = (bf16[72,2152]{1,0:T(8,128)(2,1)}, bf16[72,2152]{1,0:T(8,128)(2,1)}, u32[]{:S(2)}, u32[]{:S(2)}) collective-permute-start(bf16[72,2152]{1,0:T(8,128)(2,1)} %collective-permute-done.37), channel_id=1, source_target_pairs={{0,2},{2,4},{4,6},{6,8},{8,10},{10,12},{12,14},{14,16},{16,18},{18... | collective-permute-start | bytes 929672 | tf_op jit(solution)/shard_map/ppermute | solution.py:29
  219.8 201.6 %collective-permute-start.68 = (bf16[368,1152]{1,0:T(8,128)(2,1)}, bf16[368,1152]{1,0:T(8,128)(2,1)}, u32[]{:S(2)}, u32[]{:S(2)}) collective-permute-start(bf16[368,1152]{1,0:T(8,128)(2,1)} %get-tuple-element.79), channel_id=1, source_target_pairs={{0,1},{1,0},{2,3},{3,2},{4,5},{5,4},{6,7},{7,6},{8,9},{9,8},{10,11... | collective-permute-start | bytes 2543624 | tf_op jit(solution)/shard_map/ppermute | solution.py:139
  220.3 74.9 %collective-permute-start.61 = (bf16[72,2152]{1,0:T(8,128)(2,1)}, bf16[72,2152]{1,0:T(8,128)(2,1)}, u32[]{:S(2)}, u32[]{:S(2)}) collective-permute-start(bf16[72,2152]{1,0:T(8,128)(2,1)} %collective-permute-done.60), channel_id=1, source_target_pairs={{2,0},{4,2},{6,4},{8,6},{10,8},{12,10},{14,12},{16,14},{18,16},{20... | collective-permute-start | bytes 929672 | tf_op jit(solution)/shard_map/ppermute | solution.py:31
  220.8 76.0 %collective-permute-start.46 = (bf16[72,2152]{1,0:T(8,128)(2,1)}, bf16[72,2152]{1,0:T(8,128)(2,1)}, u32[]{:S(2)}, u32[]{:S(2)}) collective-permute-start(bf16[72,2152]{1,0:T(8,128)(2,1)} %collective-permute-done.45), channel_id=1, source_target_pairs={{2,0},{4,2},{6,4},{8,6},{10,8},{12,10},{14,12},{16,14},{18,16},{20... | collective-permute-start | bytes 929672 | tf_op jit(solution)/shard_map/ppermute | solution.py:31
  221.5 78.9 %collective-permute-start.54 = (bf16[72,2152]{1,0:T(8,128)(2,1)}, bf16[72,2152]{1,0:T(8,128)(2,1)}, u32[]{:S(2)}, u32[]{:S(2)}) collective-permute-start(bf16[72,2152]{1,0:T(8,128)(2,1)} %collective-permute-done.53), channel_id=1, source_target_pairs={{0,2},{2,4},{4,6},{6,8},{8,10},{10,12},{12,14},{14,16},{16,18},{18... | collective-permute-start | bytes 929672 | tf_op jit(solution)/shard_map/ppermute | solution.py:29
  222.6 70.8 %collective-permute-start.39 = (bf16[72,2152]{1,0:T(8,128)(2,1)}, bf16[72,2152]{1,0:T(8,128)(2,1)}, u32[]{:S(2)}, u32[]{:S(2)}) collective-permute-start(bf16[72,2152]{1,0:T(8,128)(2,1)} %collective-permute-done.38), channel_id=1, source_target_pairs={{0,2},{2,4},{4,6},{6,8},{8,10},{10,12},{12,14},{14,16},{16,18},{18... | collective-permute-start | bytes 929672 | tf_op jit(solution)/shard_map/ppermute | solution.py:29
  293.4 9.4 %collective-permute-start.40 = (bf16[72,2152]{1,0:T(8,128)(2,1)}, bf16[72,2152]{1,0:T(8,128)(2,1)S(1)}, u32[]{:S(2)}, u32[]{:S(2)}) collective-permute-start(bf16[72,2152]{1,0:T(8,128)(2,1)} %collective-permute-done.39), channel_id=1, source_target_pairs={{0,2},{2,4},{4,6},{6,8},{8,10},{10,12},{12,14},{14,16},{16,18},{18... | collective-permute-start | bytes 929672 | tf_op jit(solution)/shard_map/ppermute | solution.py:29
  295.2 99.8 %collective-permute-start.69 = (bf16[368,1152]{1,0:T(8,128)(2,1)}, bf16[368,1152]{1,0:T(8,128)(2,1)}, u32[]{:S(2)}, u32[]{:S(2)}) collective-permute-start(bf16[368,1152]{1,0:T(8,128)(2,1)} %get-tuple-element.80), channel_id=1, source_target_pairs={{0,1},{1,0},{2,3},{3,2},{4,5},{5,4},{6,7},{7,6},{8,9},{9,8},{10,11... | collective-permute-start | bytes 2543624 | tf_op jit(solution)/shard_map/ppermute | solution.py:139
  296.8 75.0 %collective-permute-start.62 = (bf16[72,2152]{1,0:T(8,128)(2,1)}, bf16[72,2152]{1,0:T(8,128)(2,1)}, u32[]{:S(2)}, u32[]{:S(2)}) collective-permute-start(bf16[72,2152]{1,0:T(8,128)(2,1)} %collective-permute-done.61), channel_id=1, source_target_pairs={{2,0},{4,2},{6,4},{8,6},{10,8},{12,10},{14,12},{16,14},{18,16},{20... | collective-permute-start | bytes 929672 | tf_op jit(solution)/shard_map/ppermute | solution.py:31
  300.5 64.7 %collective-permute-start.47 = (bf16[72,2152]{1,0:T(8,128)(2,1)}, bf16[72,2152]{1,0:T(8,128)(2,1)S(1)}, u32[]{:S(2)}, u32[]{:S(2)}) collective-permute-start(bf16[72,2152]{1,0:T(8,128)(2,1)} %collective-permute-done.46), channel_id=1, source_target_pairs={{2,0},{4,2},{6,4},{8,6},{10,8},{12,10},{14,12},{16,14},{18,16},{20... | collective-permute-start | bytes 929672 | tf_op jit(solution)/shard_map/ppermute | solution.py:31
  302.9 12.8 %collective-permute-start.55 = (bf16[72,2152]{1,0:T(8,128)(2,1)}, bf16[72,2152]{1,0:T(8,128)(2,1)S(1)}, u32[]{:S(2)}, u32[]{:S(2)}) collective-permute-start(bf16[72,2152]{1,0:T(8,128)(2,1)} %collective-permute-done.54), channel_id=1, source_target_pairs={{0,2},{2,4},{4,6},{6,8},{8,10},{10,12},{12,14},{14,16},{16,18},{18... | collective-permute-start | bytes 929672 | tf_op jit(solution)/shard_map/ppermute | solution.py:29
  315.6 22.7 %collective-permute-start.31 = (bf16[368,1152]{1,0:T(8,128)(2,1)S(1)}, bf16[368,1152]{1,0:T(8,128)(2,1)S(1)}, u32[]{:S(2)}, u32[]{:S(2)}) collective-permute-start(bf16[368,1152]{1,0:T(8,128)(2,1)S(1)} %convolution_convert_fusion.10), channel_id=1, source_target_pairs={{0,1},{1,0},{2,3},{3,2},{4,5},{5,4},{6,7},{7,6},{8,9},{9,8},{10,11... | collective-permute-start | bytes 2543624 | tf_op jit(solution)/shard_map/ppermute | solution.py:139
  338.3 21.5 %collective-permute-start.65 = (bf16[368,1152]{1,0:T(8,128)(2,1)S(1)}, bf16[368,1152]{1,0:T(8,128)(2,1)S(1)}, u32[]{:S(2)}, u32[]{:S(2)}) collective-permute-start(bf16[368,1152]{1,0:T(8,128)(2,1)S(1)} %convolution_convert_fusion.8), channel_id=1, source_target_pairs={{0,1},{1,0},{2,3},{3,2},{4,5},{5,4},{6,7},{7,6},{8,9},{9,8},{10,11... | collective-permute-start | bytes 2543624 | tf_op jit(solution)/shard_map/ppermute | solution.py:139
  362.9 22.1 %collective-permute-start.66 = (bf16[368,1152]{1,0:T(8,128)(2,1)S(1)}, bf16[368,1152]{1,0:T(8,128)(2,1)}, u32[]{:S(2)}, u32[]{:S(2)}) collective-permute-start(bf16[368,1152]{1,0:T(8,128)(2,1)S(1)} %get-tuple-element.96), channel_id=1, source_target_pairs={{0,1},{1,0},{2,3},{3,2},{4,5},{5,4},{6,7},{7,6},{8,9},{9,8},{10,11... | collective-permute-start | bytes 2543624 | tf_op jit(solution)/shard_map/ppermute | solution.py:139
  379.3 30.8 %collective-permute-start.32 = (bf16[368,1152]{1,0:T(8,128)(2,1)S(1)}, bf16[368,1152]{1,0:T(8,128)(2,1)S(1)}, u32[]{:S(2)}, u32[]{:S(2)}) collective-permute-start(bf16[368,1152]{1,0:T(8,128)(2,1)S(1)} %get-tuple-element.95), channel_id=1, source_target_pairs={{0,1},{1,0},{2,3},{3,2},{4,5},{5,4},{6,7},{7,6},{8,9},{9,8},{10,11... | collective-permute-start | bytes 2543624 | tf_op jit(solution)/shard_map/ppermute | solution.py:139
  408.1 71.8 %collective-permute-start.71 = (bf16[368,1152]{1,0:T(8,128)(2,1)}, bf16[368,1152]{1,0:T(8,128)(2,1)}, u32[]{:S(2)}, u32[]{:S(2)}) collective-permute-start(bf16[368,1152]{1,0:T(8,128)(2,1)} %convolution_convert_fusion.5), channel_id=1, source_target_pairs={{0,1},{1,0},{2,3},{3,2},{4,5},{5,4},{6,7},{7,6},{8,9},{9,8},{10,11... | collective-permute-start | bytes 2543624 | tf_op jit(solution)/shard_map/ppermute | solution.py:139
  435.3 51.4 %collective-permute-start.70 = (bf16[368,1152]{1,0:T(8,128)(2,1)}, bf16[368,1152]{1,0:T(8,128)(2,1)}, u32[]{:S(2)}, u32[]{:S(2)}) collective-permute-start(bf16[368,1152]{1,0:T(8,128)(2,1)} %convolution_convert_fusion.6), channel_id=1, source_target_pairs={{0,1},{1,0},{2,3},{3,2},{4,5},{5,4},{6,7},{7,6},{8,9},{9,8},{10,11... | collective-permute-start | bytes 2543624 | tf_op jit(solution)/shard_map/ppermute | solution.py:139
  499.6 21.9 %collective-permute-start.74 = (bf16[368,1152]{1,0:T(8,128)(2,1)S(1)}, bf16[368,1152]{1,0:T(8,128)(2,1)S(1)}, u32[]{:S(2)}, u32[]{:S(2)}) collective-permute-start(bf16[368,1152]{1,0:T(8,128)(2,1)S(1)} %convert_element_type.297), channel_id=1, source_target_pairs={{0,1},{1,0},{2,3},{3,2},{4,5},{5,4},{6,7},{7,6},{8,9},{9,8},{10,11... | collective-permute-start | bytes 2543624 | tf_op jit(solution)/shard_map/ppermute | solution.py:139
  501.7 61.6 %collective-permute-start.72 = (bf16[368,1152]{1,0:T(8,128)(2,1)S(1)}, bf16[368,1152]{1,0:T(8,128)(2,1)S(1)}, u32[]{:S(2)}, u32[]{:S(2)}) collective-permute-start(bf16[368,1152]{1,0:T(8,128)(2,1)S(1)} %convert_element_type.281), channel_id=1, source_target_pairs={{0,1},{1,0},{2,3},{3,2},{4,5},{5,4},{6,7},{7,6},{8,9},{9,8},{10,11... | collective-permute-start | bytes 2543624 | tf_op jit(solution)/shard_map/ppermute | solution.py:139
  593.0 177.2 %reduce-scatter.11.cloned.1.call-start = ((), (), s32[]{:S(2)}) async-start(), calls=%async_computation.4 | async-start | bytes 4386816 | tf_op jit(solution)/shard_map/reduce_scatter | solution.py:163
  629.0 177.0 %reduce-scatter.17.cloned.1.call-start = ((), (), s32[]{:S(2)}) async-start(), calls=%async_computation.7 | async-start | bytes 5326848
  629.8 257.6 %reduce-scatter.15.cloned.1.call-start = ((), (), s32[]{:S(2)}) async-start(), calls=%async_computation.6 | async-start | bytes 5326848
  638.1 22.1 %collective-permute-start.67 = (bf16[368,1152]{1,0:T(8,128)(2,1)}, bf16[368,1152]{1,0:T(8,128)(2,1)}, u32[]{:S(2)}, u32[]{:S(2)}) collective-permute-start(bf16[368,1152]{1,0:T(8,128)(2,1)} %convolution_convert_fusion.7), channel_id=1, source_target_pairs={{0,1},{1,0},{2,3},{3,2},{4,5},{5,4},{6,7},{7,6},{8,9},{9,8},{10,11... | collective-permute-start | bytes 2543624 | tf_op jit(solution)/shard_map/ppermute | solution.py:139
  645.8 26.2 %collective-permute-start.63 = (bf16[368,1152]{1,0:T(8,128)(2,1)}, bf16[368,1152]{1,0:T(8,128)(2,1)}, u32[]{:S(2)}, u32[]{:S(2)}) collective-permute-start(bf16[368,1152]{1,0:T(8,128)(2,1)} %convolution_convert_fusion.9), channel_id=1, source_target_pairs={{0,1},{1,0},{2,3},{3,2},{4,5},{5,4},{6,7},{7,6},{8,9},{9,8},{10,11... | collective-permute-start | bytes 2543624 | tf_op jit(solution)/shard_map/ppermute | solution.py:139
  685.0 28.6 %collective-permute-start.75 = (bf16[368,1152]{1,0:T(8,128)(2,1)S(1)}, bf16[368,1152]{1,0:T(8,128)(2,1)S(1)}, u32[]{:S(2)}, u32[]{:S(2)}) collective-permute-start(bf16[368,1152]{1,0:T(8,128)(2,1)S(1)} %convolution_convert_fusion.3), channel_id=1, source_target_pairs={{0,1},{1,0},{2,3},{3,2},{4,5},{5,4},{6,7},{7,6},{8,9},{9,8},{10,11... | collective-permute-start | bytes 2543624 | tf_op jit(solution)/shard_map/ppermute | solution.py:139
  688.0 29.5 %collective-permute-start.73 = (bf16[368,1152]{1,0:T(8,128)(2,1)S(1)}, bf16[368,1152]{1,0:T(8,128)(2,1)S(1)}, u32[]{:S(2)}, u32[]{:S(2)}) collective-permute-start(bf16[368,1152]{1,0:T(8,128)(2,1)S(1)} %convolution_convert_fusion.4), channel_id=1, source_target_pairs={{0,1},{1,0},{2,3},{3,2},{4,5},{5,4},{6,7},{7,6},{8,9},{9,8},{10,11... | collective-permute-start | bytes 2543624 | tf_op jit(solution)/shard_map/ppermute | solution.py:139
  (129 other events, 1566.8 us)
Sparse Core Ops, SparseCore 0:
  593.1 56.3 reduce-scatter.12
  653.4 70.9 reduce-scatter.10
  728.4 77.5 reduce-scatter.16
  810.4 76.9 reduce-scatter.14
